TPU v7x, 256 devices: a whole 4x4x8 slice. The times are simulated.
256 devices in a mesh: pipe: 32 (over y, z), dp: 8 (over x, core).
Axes of the slice: x: 4, y: 4, z: 8, core: 2. Of those that a mesh axis runs over, the one named last changes fastest.
Arguments:
- act_in: bfloat16 [8, 32, 128, 8192], P('dp', 'pipe'), may hold values from -6 to 6
- stash_a: bfloat16 [8, 32, 128, 8192], P('dp', 'pipe'), may hold values from -6 to 6
- grad_in: bfloat16 [8, 32, 128, 8192], P('dp', 'pipe'), may hold values from -6 to 6
- text_emb: bfloat16 [8, 128, 8192], P('dp', None, 'pipe'), may hold values from -6 to 6
- enc_query: bfloat16 [8, 128, 3200], P('dp', 'pipe'), may hold values from -32 to 32
- enc_key: bfloat16 [8, 2048, 3200], P('dp', 'pipe'), may hold values from -32 to 32
- enc_value: bfloat16 [8, 2048, 3200], P('dp', 'pipe'), may hold values from -6 to 6
- tok_count: int32 [8, 32], P('dp', 'pipe'), may hold values from 1 to 4, as said below
- tok_offset: int32 [8, 32], P('dp', 'pipe'), may hold values from 0 to 124, as said below
- merge_gain: float32 [3200], replicated, may hold values from 0.1 to 1.9
- w_merge: bfloat16 [3200, 128], P(None, 'dp'), may hold values from -0.109375 to 0.109375
- w_vision: bfloat16 [128, 8192], P(None, 'pipe'), may hold values from -0.5 to 0.5
- norm_gain: float32 [32, 8192], P('pipe'), may hold values from 0.1 to 1.9
- w_down: bfloat16 [32, 8192, 128], P('pipe', 'dp'), may hold values from -0.0625 to 0.0625
- w_up: bfloat16 [32, 128, 8192], P('pipe', None, 'dp'), may hold values from -0.5 to 0.5
Outputs:
- fwd_out: bfloat16 [8, 32, 128, 8192], P('dp', 'pipe')
- bwd_out: bfloat16 [8, 32, 128, 8192], P('dp', 'pipe')
- grad_down: float32 [32, 8192, 128], P('pipe', 'dp')
- grad_up: float32 [32, 128, 8192], P('pipe', None, 'dp')
Inputs may be any that keep to these rules, and one draw needn't show every extreme that they name: `tok_count`: in every replica some section has exactly 4 image tokens. Section p's tokens occupy positions tok_offset to tok_offset + tok_count - 1; these ranges lie within the sequence, are disjoint and rise with p.
All inputs are finite; a program needn't handle non-finite values.
Results may differ from a plain program's by a relative error of at most 0.017.
Values may be sent and summed in bfloat16 or wider, within the bound.
A program may use at most 128 MiB of HBM per device.

v0:
```python
import jax
import jax.numpy as jnp
from jax import lax
from jax.sharding import PartitionSpec as P

HEADS = 25
HEAD_DIM = 128


EPS = 1e-06


def passed_along(array, axis, by):
    length = lax.axis_size(axis)
    pairs = [(i, i + by) for i in range(length) if 0 <= i + by < length]
    return lax.ppermute(array, axis, pairs)


def swish(inner):
    return inner * jax.nn.sigmoid(inner)


def adapter_forward(x, gain, w_down, w_up):
    x32 = x.astype(jnp.float32)
    scale = lax.rsqrt(jnp.mean(x32 * x32, -1, keepdims=True) + EPS)
    normed = (x32 * scale * gain).astype(jnp.bfloat16)
    hidden = swish(jnp.dot(normed, w_down, preferred_element_type=jnp.float32)).astype(jnp.bfloat16)
    return (x32 + jnp.dot(hidden, w_up, preferred_element_type=jnp.float32)).astype(jnp.bfloat16)


def adapter_backward(x, grad_out, gain, w_down, w_up):
    x32 = x.astype(jnp.float32)
    scale = lax.rsqrt(jnp.mean(x32 * x32, -1, keepdims=True) + EPS)
    unit = x32 * scale
    normed = (unit * gain).astype(jnp.bfloat16)
    inner = jnp.dot(normed, w_down, preferred_element_type=jnp.float32)
    sig = jax.nn.sigmoid(inner)
    hidden = (inner * sig).astype(jnp.bfloat16)
    back_h = jnp.einsum("sd,rd->sr", grad_out, w_up, preferred_element_type=jnp.float32)
    back_u = (back_h * sig * (1.0 + inner * (1.0 - sig))).astype(jnp.bfloat16)
    back_n = jnp.einsum("sr,dr->sd", back_u, w_down, preferred_element_type=jnp.float32) * gain
    back_x = scale * (back_n - unit * jnp.mean(back_n * unit, -1, keepdims=True))
    grad_x = (grad_out.astype(jnp.float32) + back_x).astype(jnp.bfloat16)
    return (grad_x, normed, back_u, hidden)


def local_terms(normed, back_u, hidden, grad_out):
    down_term = jnp.einsum("sd,sr->dr", normed, back_u, preferred_element_type=jnp.float32)
    up_term = jnp.einsum("sr,sd->rd", hidden, grad_out, preferred_element_type=jnp.float32)
    return (down_term, up_term)


def encode_section(query, keys, values):
    q3 = query.reshape(query.shape[0], HEADS, HEAD_DIM)
    k3 = keys.reshape(keys.shape[0], HEADS, HEAD_DIM)
    v3 = values.reshape(values.shape[0], HEADS, HEAD_DIM)
    scores = jnp.einsum("qhd,khd->hqk", q3, k3, preferred_element_type=jnp.float32) * HEAD_DIM ** (
        -0.5
    )
    top = jnp.max(scores, -1, keepdims=True)
    weights = jnp.exp(scores - top)
    probs = (weights / jnp.sum(weights, -1, keepdims=True)).astype(jnp.bfloat16)
    attended = jnp.einsum("hqk,khd->qhd", probs, v3, preferred_element_type=jnp.float32)
    return attended.reshape(query.shape[0], HEADS * HEAD_DIM).astype(jnp.bfloat16)


def merge_tokens(rows, gain, w_merge):
    x32 = rows.astype(jnp.float32)
    scale = lax.rsqrt(jnp.mean(x32 * x32, -1, keepdims=True) + EPS)
    normed = (x32 * scale * gain).astype(jnp.bfloat16)
    return jax.nn.gelu(jnp.dot(normed, w_merge, preferred_element_type=jnp.float32)).astype(
        jnp.bfloat16
    )


def place_rows(counts, offsets, seq_len, slots):
    slot_ids = jnp.arange(slots, dtype=jnp.int32)
    target = (offsets[:, None] + slot_ids[None, :]).reshape(-1)
    live = (slot_ids[None, :] < counts[:, None]).reshape(-1)
    return (jnp.arange(seq_len, dtype=jnp.int32)[:, None] == target[None, :]) & live[None, :]


def compose(vision, marked, text, w_vision):
    mapped = jnp.dot(vision, w_vision, preferred_element_type=jnp.float32)
    return jnp.where(marked[:, None], mapped, text.astype(jnp.float32)).astype(jnp.bfloat16)


def body(
    act_in,
    stash_a,
    grad_in,
    text_emb,
    enc_query,
    enc_key,
    enc_value,
    tok_count,
    tok_offset,
    merge_gain,
    w_merge,
    w_vision,
    norm_gain,
    w_down,
    w_up,
):
    section = lax.axis_index("pipe")
    is_last = section == lax.axis_size("pipe") - 1
    down_full, up_full, merge_full = (
        lax.all_gather(w_down, "dp", axis=1, tiled=True),
        lax.all_gather(w_up, "dp", axis=2, tiled=True),
        lax.all_gather(w_merge, "dp", axis=1, tiled=True),
    )
    down_full = down_full[0]
    up_full = up_full[0]
    attended = encode_section(enc_query[0], enc_key[0], enc_value[0])
    slots = attended.shape[0]
    rows_all, counts_all, offsets_all = (
        lax.all_gather(attended[None], "pipe", axis=1, tiled=True),
        lax.all_gather(tok_count, "pipe", axis=1, tiled=True),
        lax.all_gather(tok_offset, "pipe", axis=1, tiled=True),
    )
    tokens_all = merge_tokens(rows_all[0], merge_gain, merge_full)
    placed = place_rows(counts_all[0], offsets_all[0], text_emb.shape[1], slots)
    vision = jnp.dot(
        placed.astype(jnp.bfloat16), tokens_all, preferred_element_type=jnp.float32
    ).astype(jnp.bfloat16)
    marked = jnp.any(placed, 1)
    text_full, vision_map = (
        lax.all_gather(text_emb, "pipe", axis=2, tiled=True),
        lax.all_gather(w_vision, "pipe", axis=1, tiled=True),
    )
    fresh = compose(vision, marked, text_full[0], vision_map)
    gain = norm_gain[0]
    first = act_in[0, 0]
    out0 = adapter_forward(first, gain, down_full, up_full)
    before = passed_along(out0, "pipe", 1)
    incoming = jnp.where(section == 0, fresh, before)
    out1 = adapter_forward(incoming, gain, down_full, up_full)
    grad_first = lax.cond(
        is_last,
        lambda: adapter_forward(stash_a[0, 0], gain, down_full, up_full),
        lambda: grad_in[0, 0],
    )
    back0, normed0, factor0, hidden0 = adapter_backward(
        stash_a[0, 0], grad_first, gain, down_full, up_full
    )
    after = passed_along(back0, "pipe", -1)
    grad_second = jnp.where(is_last, out0, after)
    back1, normed1, factor1, hidden1 = adapter_backward(
        first, grad_second, gain, down_full, up_full
    )
    down0, up0 = local_terms(normed0, factor0, hidden0, grad_first)
    down1, up1 = local_terms(normed1, factor1, hidden1, grad_second)
    grad_down, grad_up = (
        lax.psum_scatter(
            (down0 + down1)[None].astype(jnp.bfloat16), "dp", scatter_dimension=1, tiled=True
        ).astype(jnp.float32),
        lax.psum_scatter(
            (up0 + up1)[None].astype(jnp.bfloat16), "dp", scatter_dimension=2, tiled=True
        ).astype(jnp.float32),
    )
    return (out1[None, None], back1[None, None], grad_down, grad_up)


def solution(mesh):
    in_specs = (
        P("dp", "pipe", None, None),
        P("dp", "pipe", None, None),
        P("dp", "pipe", None, None),
        P("dp", None, "pipe"),
        P("dp", "pipe", None),
        P("dp", "pipe", None),
        P("dp", "pipe", None),
        P("dp", "pipe"),
        P("dp", "pipe"),
        P(),
        P(None, "dp"),
        P(None, "pipe"),
        P("pipe", None),
        P("pipe", "dp", None),
        P("pipe", None, "dp"),
    )
    out_specs = (
        P("dp", "pipe", None, None),
        P("dp", "pipe", None, None),
        P("pipe", "dp", None),
        P("pipe", None, "dp"),
    )
    return jax.shard_map(body, mesh=mesh, in_specs=in_specs, out_specs=out_specs, check_vma=False)
```

profile of v0, /device:TPU:1, one launch (start us, length us, event | category | flops | bytes accessed | tf_op | source)
XLA Modules:
  0.0 317.2 jit_solution(1194852371603357867)
XLA Ops:
  7.2 3.2 %copy.58 = bf16[1,1,128,8192]{3,2,1,0:T(8,128)(2,1)} copy(bf16[1,1,128,8192]{3,2,1,0:T(8,128)(2,1)} %param.19) | data formatting | bytes 4194304
  13.1 29.4 %all-gather.9.cloned.1.call-done = bf16[1,8192,128]{2,1,0:T(8,128)(2,1)} async-done(((bf16[1,1024,128]{2,1,0:T(8,128)(2,1)}), bf16[1,8192,128]{2,1,0:T(8,128)(2,1)}) %all-gather.9.cloned.1.call-update) | async-done | bytes 2097168 | tf_op jit(solution)/shard_map/all_gather | solution.py:108
  42.6 29.9 %all-gather.11.cloned.1.call-done = bf16[1,128,8192]{2,1,0:T(8,128)(2,1)} async-done(((bf16[1,128,1024]{2,1,0:T(8,128)(2,1)}), bf16[1,128,8192]{2,1,0:T(8,128)(2,1)}) %all-gather.11.cloned.1.call-update) | async-done | bytes 2097168 | tf_op jit(solution)/shard_map/all_gather | solution.py:109
  72.5 2.6 fusion.56
  76.9 1.0 fusion.45
  78.0 1.2 fusion.49
  79.2 1.3 collective-permute-start.1
  82.8 49.1 %collective-permute-done.1 = bf16[128,8192]{1,0:T(8,128)(2,1)S(1)} collective-permute-done((bf16[128,8192]{1,0:T(8,128)(2,1)S(1)}, bf16[128,8192]{1,0:T(8,128)(2,1)S(1)}, u32[]{:S(2)}, u32[]{:S(2)}) %collective-permute-start.1) | collective-permute-done | bytes 2097184 | tf_op jit(solution)/shard_map/ppermute | solution.py:16
  131.8 2.5 broadcast_select_fusion
  135.7 2.5 fusion.22
  140.7 48.1 %all_gather.26 = bf16[1,128,3200]{2,0,1:T(2,128)(2,1)S(1)} all-gather(bf16[1,4,3200]{2,0,1:T(2,128)(2,1)S(1)} %copy.36), channel_id=1, replica_groups=mesh['pipe'=32,'dp'=8] {'pipe'}, dimensions={1}, use_global_device_ids=true | all-gather | bytes 844800 | tf_op jit(solution)/shard_map/all_gather | solution.py:117
  188.8 2.9 convert_element_type.207
  195.1 12.8 %all-reduce.2 = (s32[32]{0:T(128)S(1)}, s32[32]{0:T(128)S(1)}) all-reduce(s32[32]{0:T(128)S(1)} %bitcast_dynamic-update-slice_fusion.1, s32[32]{0:T(128)S(1)} %bitcast_dynamic-update-slice_fusion), channel_id=1, replica_groups=mesh['pipe'=32,'dp'=8] {'pipe'}, use_global_device_ids=true, to_apply=%add | all-reduce | flops 64 | bytes 512
  208.4 1.6 fusion.75
  210.0 29.0 %all_gather.27 = bf16[3200,128]{0,1:T(8,128)(2,1)S(1)} all-gather(bf16[3200,16]{0,1:T(8,128)(2,1)S(1)} %copy-done.16), channel_id=1, replica_groups=mesh['pipe'=32,'dp'=8] {'dp'}, dimensions={1}, use_global_device_ids=true | all-gather | bytes 921600 | tf_op jit(solution)/shard_map/all_gather | solution.py:110
  240.6 2.1 fusion.21
  243.4 2.0 fusion.100
  245.4 5.0 %collective-permute-start = (bf16[128,8192]{1,0:T(8,128)(2,1)}, bf16[128,8192]{1,0:T(8,128)(2,1)}, u32[]{:S(2)}, u32[]{:S(2)}) collective-permute-start(bf16[128,8192]{1,0:T(8,128)(2,1)} %get-tuple-element.33), channel_id=1, source_target_pairs={{0,8},{8,16},{16,24},{24,32},{32,40},{40,48},{48,56},{56,64},{64,7... | collective-permute-start | bytes 6291464 | tf_op jit(solution)/shard_map/ppermute | solution.py:16
  251.5 2.6 fusion.64
  254.0 40.2 %collective-permute-done = bf16[128,8192]{1,0:T(8,128)(2,1)} collective-permute-done((bf16[128,8192]{1,0:T(8,128)(2,1)}, bf16[128,8192]{1,0:T(8,128)(2,1)}, u32[]{:S(2)}, u32[]{:S(2)}) %collective-permute-start) | collective-permute-done | bytes 2097184 | tf_op jit(solution)/shard_map/ppermute | solution.py:16
  294.3 5.6 %multiply_reduce_fusion = (f32[128]{0:T(128)S(1)}, f32[128,8192]{1,0:T(8,128)}) fusion(bf16[128,8192]{1,0:T(8,128)(2,1)} %collective-permute-done, bf16[1,128,8192]{2,1,0:T(8,128)(2,1)} %all-gather.7.cloned.1.call-done, bf16[128,8192]{1,0:T(8,128)(2,1)} %all-gather.5.cloned.1.call-done, bf16[128,128]{1,0:T(8,128)(2,1)S(1)} %fusion.100, s32[128]{0:T(128)S(1)} %add.119, ...), kind=kOutput, calls=%fused_computation.66 | convolution fusion | flops 280018816 | bytes 10519809 | tf_op jit(solution)/shard_map/dot_general | solution.py:84
  299.9 6.9 %fusion.23 = bf16[1,1,128,8192]{3,2,1,0:T(8,128)(2,1)} fusion(f32[128,8192]{1,0:T(8,128)} %get-tuple-element.29, f32[8192]{0:T(1024)S(1)} %bitcast.167, f32[128]{0:T(128)S(1)} %add_rsqrt_fusion.2, bf16[1,128,8192]{2,1,0:T(8,128)(2,1)S(1)} %copy-done.5, bf16[1,8192,128]{2,1,0:T(8,128)(2,1)} %all-gather.9.cloned.1.call-done), kind=kOutput, calls=%fused_computation.30 | convolution fusion | flops 542195712 | bytes 10519040 | tf_op jit(solution)/shard_map/dot_general | solution.py:28
  306.8 1.8 convert_element_type.201
  308.6 1.8 convert_element_type.205
  (85 shorter events, 16.2 us)
Async XLA Ops:
  7.2 132.4 %copy-start = (bf16[1,4,3200]{2,1,0:T(4,128)(2,1)S(1)}, bf16[1,4,3200]{2,1,0:T(4,128)(2,1)}, u32[]{:S(2)}) copy-start(bf16[1,4,3200]{2,1,0:T(4,128)(2,1)} %param.21) | copy-start | bytes 76804
  7.2 35.4 %all-gather.9.cloned.1.call-start = ((), (), s32[]{:S(2)}) async-start(), calls=%async_computation.4 | async-start | bytes 2359296 | tf_op jit(solution)/shard_map/all_gather | solution.py:108
  7.2 5.4 %copy-start.1 = (bf16[1,1,128,8192]{3,2,1,0:T(8,128)(2,1)S(1)}, bf16[1,1,128,8192]{3,2,1,0:T(8,128)(2,1)}, u32[]{:S(2)}) copy-start(bf16[1,1,128,8192]{3,2,1,0:T(8,128)(2,1)} %param.18) | copy-start | bytes 6291460
  10.5 62.0 %copy-start.13 = (f32[1,8192]{1,0:T(1,128)S(1)}, f32[1,8192]{1,0:T(1,128)}, u32[]{:S(2)}) copy-start(f32[1,8192]{1,0:T(1,128)} %param.29) | copy-start | bytes 98308
  10.5 62.0 %all-gather.11.cloned.1.call-start = ((), (), s32[]{:S(2)}) async-start(), calls=%async_computation.5 | async-start | bytes 2359296 | tf_op jit(solution)/shard_map/all_gather | solution.py:109
  11.3 242.8 %all-gather.7.cloned.1.call-start = ((), (), s32[]{:S(2)}) async-start(), calls=%async_computation.3 | async-start | bytes 2162688 | tf_op jit(solution)/shard_map/all_gather | solution.py:128
  12.0 242.0 %all-gather.5.cloned.1.call-start = ((), (), s32[]{:S(2)}) async-start(), calls=%async_computation.2 | async-start | bytes 2162688 | tf_op jit(solution)/shard_map/all_gather | solution.py:129
  12.6 294.2 %reduce-scatter.3.cloned.1.call-start = ((), (), s32[]{:S(2)}) async-start(), calls=%async_computation.6 | async-start | bytes 2359296 | tf_op jit(solution)/shard_map/reduce_scatter | solution.py:154
  72.5 2.6 copy-start.4
  72.5 2.9 copy-start.8
  75.3 1.6 copy-start.6
  78.0 2.6 copy-start.2
  79.2 52.6 %collective-permute-start.1 = (bf16[128,8192]{1,0:T(8,128)(2,1)S(1)}, bf16[128,8192]{1,0:T(8,128)(2,1)S(1)}, u32[]{:S(2)}, u32[]{:S(2)}) collective-permute-start(bf16[128,8192]{1,0:T(8,128)(2,1)S(1)} %fusion.49), channel_id=1, source_target_pairs={{8,0},{16,8},{24,16},{32,24},{40,32},{48,40},{56,48},{64,56},{72,6... | collective-permute-start | bytes 6291464 | tf_op jit(solution)/shard_map/ppermute | solution.py:16
  134.3 1.3 copy-start.10
  138.2 170.4 %reduce-scatter.5.cloned.1.call-start = ((), (), s32[]{:S(2)}) async-start(), calls=%async_computation.7 | async-start | bytes 2359296 | tf_op jit(solution)/shard_map/reduce_scatter | solution.py:157
  140.7 52.4 %copy-start.18 = (u32[256]{0:T(256)S(1)}, u32[256]{0:T(256)}, u32[]{:S(2)}) copy-start(u32[256]{0:T(256)} %constant.61) | copy-start | bytes 3076
  188.8 21.2 %copy-start.16 = (bf16[3200,16]{0,1:T(8,128)(2,1)S(1)}, bf16[3200,16]{0,1:T(8,128)(2,1)}, u32[]{:S(2)}) copy-start(bf16[3200,16]{0,1:T(8,128)(2,1)} %param.27) | copy-start | bytes 307204
  191.7 47.3 %copy-start.9 = (bf16[128,8192]{1,0:T(8,128)(2,1)S(1)}, bf16[128,8192]{1,0:T(8,128)(2,1)}, u32[]{:S(2)}) copy-start(bf16[128,8192]{1,0:T(8,128)(2,1)} %get-tuple-element.37) | copy-start | bytes 6291460
  239.0 1.6 copy-start.11
  242.7 7.8 %copy-start.3 = (bf16[1,1,128,8192]{3,2,1,0:T(8,128)(2,1)S(1)}, bf16[1,1,128,8192]{3,2,1,0:T(8,128)(2,1)}, u32[]{:S(2)}) copy-start(bf16[1,1,128,8192]{3,2,1,0:T(8,128)(2,1)} %param.17) | copy-start | bytes 6291460
  243.4 7.0 %copy-start.7 = (bf16[1,8192,128]{2,1,0:T(8,128)(2,1)S(1)}, bf16[1,8192,128]{2,1,0:T(8,128)(2,1)}, u32[]{:S(2)}) copy-start(bf16[1,8192,128]{2,1,0:T(8,128)(2,1)} %all-gather.9.cloned.1.call-done) | copy-start | bytes 6291460
  245.4 6.0 %copy-start.12 = (bf16[128,8192]{1,0:T(8,128)(2,1)S(1)}, bf16[128,8192]{1,0:T(8,128)(2,1)}, u32[]{:S(2)}) copy-start(bf16[128,8192]{1,0:T(8,128)(2,1)} %copy-done.10) | copy-start | bytes 6291460
  245.4 48.8 %collective-permute-start = (bf16[128,8192]{1,0:T(8,128)(2,1)}, bf16[128,8192]{1,0:T(8,128)(2,1)}, u32[]{:S(2)}, u32[]{:S(2)}) collective-permute-start(bf16[128,8192]{1,0:T(8,128)(2,1)} %get-tuple-element.33), channel_id=1, source_target_pairs={{0,8},{8,16},{16,24},{24,32},{32,40},{40,48},{48,56},{56,64},{64,7... | collective-permute-start | bytes 6291464 | tf_op jit(solution)/shard_map/ppermute | solution.py:16
  254.0 45.8 %copy-start.5 = (bf16[1,128,8192]{2,1,0:T(8,128)(2,1)S(1)}, bf16[1,128,8192]{2,1,0:T(8,128)(2,1)}, u32[]{:S(2)}) copy-start(bf16[1,128,8192]{2,1,0:T(8,128)(2,1)} %all-gather.11.cloned.1.call-done) | copy-start | bytes 6291460
  (3 other events, 2.9 us)
Sparse Core Ops, SparseCore 0:
  10.6 31.8 all-gather.8
  44.4 28.0 all-gather.10
  74.9 79.6 all-gather.6
  157.0 73.7 all-gather.4
  233.1 35.8 reduce-scatter.2
  271.4 36.0 reduce-scatter.4
where the time goes:
time: 319 us; the launch traced here: 317 us
  waiting for transfers between devices  151 us (47%)
  blocking collectives  89.9 us (28%)
  matrix products  30.9 us (10%)
  between operations  15.8 us (5%)
  other arithmetic  13.4 us (4%)
  local copies, waits for them, and re-layouts  9.95 us (3%)
  starting transfers between devices  6.69 us (2%)
    ppermute x2, waiting for transfers between devices, passed_along(): return lax.ppermute(array, axis, pairs)  89.3 us
    all_gather x1, blocking collectives, body(): lax.all_gather(attended[None], 'pipe', axis=1, tiled=True)  48.1 us
    all_gather x1, waiting for transfers between devices, body(): lax.all_gather(w_up, 'dp', axis=2, tiled=True)  29.9 us
    all_gather x1, waiting for transfers between devices, body(): lax.all_gather(w_down, 'dp', axis=1, tiled=True)  29.4 us
    all_gather x1, blocking collectives, body(): lax.all_gather(w_merge, 'dp', axis=1, tiled=True)  29 us
    unnamed x1, blocking collectives  12.8 us
    dot_general x2, matrix products, adapter_forward(): jnp.dot(hidden, w_up, preferred_element_type=jnp.float32)  9.4 us
    unnamed x44, local copies, waits for them, and re-layouts  9.27 us
  transfers between devices with their start and end apart: 8, of which 4 were waited for; matrix products, arithmetic and copies ran while one was open for 14% of the time, Pallas kernels for 0%

commit v1 on v0

v1 whole, which is shorter than its diff:
```python
import functools

import jax
import jax.numpy as jnp
from jax import lax
from jax.experimental import pallas as pl
from jax.experimental.pallas import tpu as pltpu
from jax.sharding import PartitionSpec as P

HEAD_DIM = 128
EPS = 1e-06
RING = 4
Z = 8
TOK = 16
MESH = pl.DeviceIdType.MESH
BF, F32 = jnp.bfloat16, jnp.float32


def mm(a, b):
    return jnp.dot(a, b, preferred_element_type=F32)


def mm_nt(a, b):
    return lax.dot_general(a, b, (((1,), (1,)), ((), ())), preferred_element_type=F32)


def mm_tn(a, b):
    return lax.dot_general(a, b, (((0,), (0,)), ((), ())), preferred_element_type=F32)


def swish(inner):
    return inner * jax.nn.sigmoid(inner)


def pick(k, values):
    out = jnp.int32(values[-1])
    for i in range(len(values) - 2, -1, -1):
        out = jnp.where(k == i, jnp.int32(values[i]), out)
    return out


def rcopy(src, dst, send_sem, recv_sem, device):
    return pltpu.make_async_remote_copy(
        src_ref=src,
        dst_ref=dst,
        send_sem=send_sem,
        recv_sem=recv_sem,
        device_id=device,
        device_id_type=MESH,
    )


FWD = (0, 3, 1, 2)
BWD = (2, 1, 3, 0)


def kernel(
    n_pipe,
    act_h, st_h, gin_h, text_h, wv_h, q_ref, ek_h, ev_h, cnt_ref, off_ref, mg_ref, wm_h, gain_ref, wd_h, wu_h,
    fwd_h, bwd_h, gd_h, gu_h,
    X, G, N, wd, wu, xin, O0, B0, nall, but, upf, ups, upr, uxs, uxr, dps, dpr, dxs, dxr, accu, accd,
    wm, ek, ev, text, wv, scr, att, tk, fb, fra, sc, inner, sig, hid, hidt, bh, bu, ic, ss, hid2, gdo,
    ld, ags, agr, aus, aur, wms, wmr, zfs, zfr, zbs, zbr, nas, nar, bus, bur,
    ups_s, ups_r, uxs_s, uxs_r, dps_s, dps_r, dxs_s, dxs_r, tzs, tzr, tys, tyr, fzs, fzr, fys, fyr, outs,
):
    nq, s2, db = X.shape
    s = s2 // 2
    r = wu.shape[1]
    dp_cols = fb.shape[1]
    per = db // dp_cols
    n_y = n_pipe // Z
    width = nq * db
    heads = att.shape[1] // HEAD_DIM

    p, d = lax.axis_index("pipe"), lax.axis_index("dp")
    y, z = p // Z, p % Z
    x, c = d // 2, d % 2
    last = p == n_pipe - 1
    xr, xl, xo = (x + 1) % RING, (x + 3) % RING, (x + 2) % RING

    def at(chip, core):
        return chip * 2 + core

    right, left, other, mate = (p, at(xr, c)), (p, at(xl, c)), (p, at(xo, c)), (p, at(x, 1 - c))

    def cols(ref, q):
        return ref.at[:, pl.ds(pl.multiple_of(q * db, 128), db)]

    def load(i, src, dst):
        return pltpu.make_async_copy(src, dst, ld.at[i])

    small = [
        lambda: load(0, wd_h, wd.at[d]),
        lambda: load(1, wu_h, wu.at[d]),
        lambda: load(2, wm_h, wm.at[d]),
        lambda: load(3, ek_h, ek),
        lambda: load(4, ev_h, ev),
        lambda: load(5, text_h, text),
        lambda: load(6, wv_h, wv),
    ]

    def big(q):
        return (
            load(8 + q, cols(act_h, q), X.at[q, pl.ds(0, s)]),
            load(8 + nq + q, cols(st_h, q), X.at[q, pl.ds(s, s)]),
            load(8 + 2 * nq + q, cols(gin_h, q), G.at[q, pl.ds(s, s)]),
        )

    for copy in small:
        copy().start()

    def start_big(q, carry):
        for copy in big(q):
            copy.start()
        return carry

    lax.fori_loop(0, nq, start_big, 0)

    barrier = pltpu.get_barrier_semaphore()

    def greet(device):
        pl.semaphore_signal(barrier, inc=1, device_id=device, device_id_type=MESH)

    for i in range(1, nq):
        greet((p, (d + i) % nq))
    for i in range(1, Z):
        greet((y * Z + (z + i) % Z, d))
    for i in range(1, n_y):
        greet((((y + i) % n_y) * Z + z, d))
    up_wrap = (z == Z - 1) & (y < n_y - 1)
    down_wrap = (z == 0) & (y > 0)

    @pl.when(up_wrap)
    def _():
        greet((p + 1, d))

    @pl.when(down_wrap)
    def _():
        greet((p - 1, d))

    extra = jnp.where(up_wrap | down_wrap, 1, 0)
    pl.semaphore_wait(barrier, nq - 1 + Z - 1 + n_y - 1 + extra)

    class Gather:
        def __init__(self, buf, send, recv):
            self.buf, self.send, self.recv = buf, send, recv
            self.half = buf.shape[1] // 2

        def copy(self, i):
            lo, hi = pl.ds(0, self.half), pl.ds(self.half, self.half)
            ref, device = (
                lambda: (self.buf.at[d], right),
                lambda: (self.buf.at[d], left),
                lambda: (self.buf.at[at(xl, c), lo], right),
                lambda: (self.buf.at[at(xr, c), hi], left),
                lambda: (self.buf.at[d], mate),
                lambda: (self.buf.at[at(xl, c)], mate),
                lambda: (self.buf.at[at(xr, c)], mate),
                lambda: (self.buf.at[at(xo, c)], mate),
            )[i]()
            return rcopy(ref, ref, self.send.at[i], self.recv.at[i], device)

        def arrival(self, i):
            lo, hi = pl.ds(0, self.half), pl.ds(self.half, self.half)
            ref = (
                lambda: self.buf.at[at(xl, c)],
                lambda: self.buf.at[at(xr, c)],
                lambda: self.buf.at[at(xo, c), lo],
                lambda: self.buf.at[at(xo, c), hi],
                lambda: self.buf.at[at(x, 1 - c)],
                lambda: self.buf.at[at(xl, 1 - c)],
                lambda: self.buf.at[at(xr, 1 - c)],
                lambda: self.buf.at[at(xo, 1 - c)],
            )[i]()
            return rcopy(ref, ref, self.send.at[i], self.recv.at[i], mate)

        def go(self, *which):
            for i in which:
                self.copy(i).start()

        def wait(self, *which):
            for i in which:
                self.arrival(i).wait_recv()

        def drain(self):
            for i in range(8):
                self.copy(i).wait_send()

    down, up = Gather(wd, ags, agr), Gather(wu, aus, aur)

    def merge_copy(i):
        ref, device = (
            lambda: (wm.at[d], right),
            lambda: (wm.at[d], left),
            lambda: (wm.at[d], other),
            lambda: (wm.at[d], mate),
            lambda: (wm.at[at(xl, c)], mate),
            lambda: (wm.at[at(xr, c)], mate),
            lambda: (wm.at[at(xo, c)], mate),
        )[i]()
        return rcopy(ref, ref, wms.at[i], wmr.at[i], device)

    def merge_arrival(i):
        ref = (
            lambda: wm.at[at(xl, c)],
            lambda: wm.at[at(xr, c)],
            lambda: wm.at[at(xo, c)],
            lambda: wm.at[at(x, 1 - c)],
            lambda: wm.at[at(xl, 1 - c)],
            lambda: wm.at[at(xr, 1 - c)],
            lambda: wm.at[at(xo, 1 - c)],
        )[i]()
        return rcopy(ref, ref, wms.at[i], wmr.at[i], mate)

    small[0]().wait()
    down.go(0, 1, 4)
    small[1]().wait()
    small[2]().wait()

    ss[...] = jnp.zeros_like(ss)

    def squares(q, carry):
        for copy in big(q):
            copy.wait()
        v = X[q].astype(F32)
        ss[...] += jnp.sum(v * v, -1, keepdims=True)
        return carry

    lax.fori_loop(0, nq, squares, 0)
    sc[...] = lax.rsqrt(ss[...] * (1.0 / width) + EPS)

    def normalise(q, carry):
        N[q] = (X[q].astype(F32) * sc[...] * gain_ref[q]).astype(BF)
        return carry

    lax.fori_loop(0, nq, normalise, 0)

    down.wait(0)
    down.go(2, 5)
    down.wait(1)
    down.go(3, 6)
    up.go(0, 1, 4)
    for i in range(4):
        merge_copy(i).start()

    small[3]().wait()
    small[4]().wait()
    query = jnp.concatenate([q_ref[...].astype(F32), jnp.zeros((TOK - q_ref.shape[0], q_ref.shape[1]), F32)], 0)
    query = query.astype(BF)
    for h in range(heads):
        lanes = slice(h * HEAD_DIM, (h + 1) * HEAD_DIM)
        scr[h * TOK:(h + 1) * TOK] = mm_nt(query[:, lanes], ek[:, lanes]) * HEAD_DIM ** (-0.5)
    scores = scr[...]
    weights = jnp.exp(scores - jnp.max(scores, -1, keepdims=True))
    scr[...] = weights / jnp.sum(weights, -1, keepdims=True)
    for h in range(heads):
        lanes = slice(h * HEAD_DIM, (h + 1) * HEAD_DIM)
        att[:, lanes] = mm(scr[h * TOK:(h + 1) * TOK].astype(BF), ev[:, lanes])

    down.wait(2, 3)
    down.go(7)
    down.wait(4, 5, 6, 7)

    inner[...] = jnp.zeros_like(inner)

    def add_inner(q, carry):
        inner[...] += mm(N[q], wd[q])
        return carry

    lax.fori_loop(0, nq, add_inner, 0)
    sig[...] = jax.nn.sigmoid(inner[...])
    hidden = inner[...] * sig[...]
    hid[...] = hidden.astype(BF)
    hidt[...] = hidden.T.astype(BF)

    bh[...] = jnp.zeros_like(bh)

    def fwd_send(q):
        return rcopy(O0.at[q], xin.at[q], zfs.at[q], zfr.at[q], (p + 1, d))

    def bwd_send(q):
        return rcopy(B0.at[q], G.at[q, pl.ds(0, s)], zbs.at[q], zbr.at[q], (p - 1, d))

    def fwd_block(j):
        return at((x + pick(j // 2, FWD)) % RING, jnp.where(j % 2 == 0, c, 1 - c))

    def bwd_block(j):
        return at((x + pick(j // 2, BWD)) % RING, jnp.where(j % 2 == 0, 1 - c, c))

    def first_forward(j, carry):
        q = fwd_block(j)

        @pl.when(j == 1)
        def _():
            up.wait(4)

        @pl.when(j == 2)
        def _():
            up.wait(0)
            up.go(2, 5)
            up.wait(1)
            up.go(3, 6)

        @pl.when(j == 3)
        def _():
            up.wait(5)

        @pl.when(j == 5)
        def _():
            up.wait(6)

        @pl.when(j == 6)
        def _():
            up.wait(2, 3)
            up.go(7)

        @pl.when(j == 7)
        def _():
            up.wait(7)

        out = (X[q, :s].astype(F32) + mm(hid[:s], wu[q])).astype(BF)

        @pl.when(last)
        def _():
            G[q, :s] = out
            G[q, s:] = (X[q, s:].astype(F32) + mm(hid[s:], wu[q])).astype(BF)

        @pl.when(jnp.logical_not(last))
        def _():
            O0[q] = out
            fwd_send(q).start()

        bh[...] += mm_nt(G[q, s:], wu[q])
        return carry

    lax.fori_loop(0, nq, first_forward, 0)

    for i, k in ((0, 4), (1, 5), (2, 6)):
        merge_arrival(i).wait_recv()
        merge_copy(k).start()

    def factor(rows):
        sg, inn = sig[rows], inner[rows]
        value = (bh[...] * sg * (1.0 + inn * (1.0 - sg))).astype(BF)
        wide = value.astype(F32)
        return value, wide, jnp.sum(wide * inn, -1, keepdims=True) * (1.0 / width)

    hi_rows, lo_rows = slice(s, 2 * s), slice(0, s)

    bu_b, wide_b, mean_b = factor(hi_rows)
    bu[...] = bu_b
    scale_b = sc[hi_rows]
    coef_b = scale_b * mean_b

    def first_backward(j, carry):
        q = bwd_block(j)
        back = mm_nt(bu[...], wd[q]) * gain_ref[q]
        value = G[q, s:].astype(F32) + scale_b * (back - X[q, s:].astype(F32) * coef_b)

        @pl.when(p > 0)
        def _():
            B0[q] = value.astype(BF)
            bwd_send(q).start()

        return carry

    lax.fori_loop(0, nq, first_backward, 0)

    for i in range(3, 7):
        merge_arrival(i).wait_recv()
    rows = att[...].astype(BF).astype(F32)
    scale_m = lax.rsqrt(jnp.mean(rows * rows, -1, keepdims=True) + EPS)
    rows = (rows * scale_m * mg_ref[...]).astype(BF)
    tokens = jax.nn.gelu(mm_nt(rows, wm[...].reshape(nq * wm.shape[1], wm.shape[2])))
    tk[p, :TOK] = tokens.astype(BF)
    slot = lax.broadcasted_iota(jnp.int32, (TOK, s), 0)
    place = lax.broadcasted_iota(jnp.int32, (TOK, s), 1)
    live = (slot < cnt_ref[0, 0]) & (place == off_ref[0, 0] + slot)
    tk[p, TOK:] = jnp.where(live, 1.0, 0.0).astype(BF)

    def tok_z(i, slot_z):
        ref = tk.at[y * Z + slot_z]
        return rcopy(ref, ref, tzs.at[i], tzr.at[i], (y * Z + (z + i) % Z, d))

    def tok_y(i, slot_y):
        ref = tk.at[pl.ds(slot_y * Z, Z)]
        return rcopy(ref, ref, tys.at[i], tyr.at[i], (((y + i) % n_y) * Z + z, d))

    for i in range(1, Z):
        tok_z(i, z).start()

    but_b = wide_b.T.astype(BF)
    bu[...] = but_b

    def down_mate(k):
        return rcopy(dps.at[k], dpr.at[k], dps_s.at[k], dps_r.at[k], mate)

    def down_x(k):
        device = (p, at((x + pick(k, BWD)) % RING, c))
        return rcopy(dxs.at[k], dxr.at[k], dxs_s.at[k], dxs_r.at[k], device)

    def up_mate(k):
        return rcopy(ups.at[k], upr.at[k], ups_s.at[k], ups_r.at[k], mate)

    def up_x(k):
        device = (p, at((x + pick(k, BWD)) % RING, c))
        return rcopy(uxs.at[k], uxr.at[k], uxs_s.at[k], uxs_r.at[k], device)

    def down_first(k, carry):
        dps[k] = mm(bu[...], N[bwd_block(2 * k), s:]).astype(BF)
        down_mate(k).start()
        return carry

    lax.fori_loop(0, RING, down_first, 0)

    def down_second(k, carry):
        value = mm(bu[...], N[bwd_block(2 * k + 1), s:])
        down_mate(k).wait_recv()
        value = value + dpr[k].astype(F32)

        @pl.when(k < RING - 1)
        def _():
            dxs[k] = value.astype(BF)
            down_x(k).start()

        @pl.when(k == RING - 1)
        def _():
            accd[...] = value

        return carry

    lax.fori_loop(0, RING, down_second, 0)

    def norm_copy(i):
        target = (d + i) % nq
        return rcopy(N.at[target, pl.ds(0, s)], nall.at[d], nas.at[i], nar.at[i], (p, target))

    def norm_arrival(i):
        ref = nall.at[(d + nq - i) % nq]
        return rcopy(ref, ref, nas.at[i], nar.at[i], mate)

    for i in range(1, nq):
        norm_copy(i).start()
    nall[d] = N[d, :s]

    for i in range(1, Z):
        tok_z(i, (z + Z - i) % Z).wait_recv()
    for i in range(1, n_y):
        tok_y(i, y).start()
    for i in range(1, n_y):
        tok_y(i, (y + n_y - i) % n_y).wait_recv()
    small[5]().wait()
    small[6]().wait()
    held = tk[:, :TOK].reshape(n_pipe * TOK, r)
    spots = tk[:, TOK:].reshape(n_pipe * TOK, s)
    vision = mm_tn(spots, held).astype(BF)
    marked = mm_tn(spots, jnp.ones_like(held))[:, :1] > 0.5
    fresh = jnp.where(marked, mm(vision, wv[...]), text[...].astype(F32)).astype(BF)

    def fresh_z(slot):
        return rcopy(fb, fra.at[y, slot], fzs.at[0], fzr.at[slot], (y * Z, d))

    def fresh_y(slot):
        return rcopy(fra.at[y], fra.at[slot], fys.at[0], fyr.at[slot], (0, d))

    @pl.when(z == 0)
    def _():
        fra[y, 0] = fresh

    @pl.when(z > 0)
    def _():
        fb[...] = fresh
        fresh_z(z).start()

    ss[...] = jnp.zeros_like(ss)
    ic[...] = jnp.zeros_like(ic)
    bh[...] = jnp.zeros_like(bh)

    def take_forward(q):
        v = xin[q].astype(F32)
        ss[:s] += jnp.sum(v * v, -1, keepdims=True)
        ic[...] += mm((v * gain_ref[q]).astype(BF), wd[q])

    def fwd_out(q):
        return pltpu.make_async_copy(xin.at[q], cols(fwd_h, q), outs.at[q])

    def bwd_out(q):
        return pltpu.make_async_copy(G.at[q, pl.ds(0, s)], cols(bwd_h, q), outs.at[nq + q])

    def but_copy(i):
        return rcopy(but.at[d], but.at[d], bus.at[i], bur.at[i], (p, (d + i) % nq))

    def but_arrival(i):
        ref = but.at[(d + nq - i) % nq]
        return rcopy(ref, ref, bus.at[i], bur.at[i], mate)

    def second(j, carry):
        qf, qb = fwd_block(j), bwd_block(j)

        @pl.when(p > 0)
        def _():
            fwd_send(qf).wait_recv()
            take_forward(qf)

        @pl.when((j == 1) & (z == 0))
        def _():
            for i in range(1, Z):
                fresh_z(i).wait_recv()

            @pl.when(y > 0)
            def _():
                fresh_y(y).start()

        @pl.when((j == nq - 1) & (p == 0))
        def _():
            for i in range(1, n_y):
                fresh_y(i).wait_recv()

            def assemble(q, carry):
                for i in range(per):
                    sec = q * per + i
                    xin[q, :, i * dp_cols:(i + 1) * dp_cols] = fra[sec // Z, sec % Z]
                take_forward(q)
                return carry

            lax.fori_loop(0, nq, assemble, 0)

        @pl.when(j == nq - 1)
        def _():
            scale = lax.rsqrt(ss[:s] * (1.0 / width) + EPS)
            hid2[...] = swish(ic[...] * scale).astype(BF)

            def finish(q, carry):
                xin[q] = (xin[q].astype(F32) + mm(hid2[...], wu[q])).astype(BF)
                fwd_out(q).start()
                return carry

            lax.fori_loop(0, nq, finish, 0)

        @pl.when(jnp.logical_not(last))
        def _():
            bwd_send(qb).wait_recv()

        bh[...] += mm_nt(G[qb, :s], wu[qb])

        @pl.when(j == nq - 1)
        def _():
            bu_a, wide_a, mean_a = factor(lo_rows)
            but[d] = wide_a.T.astype(BF)
            for i in range(1, nq):
                but_copy(i).start()
            bu[...] = bu_a
            ss[:s] = mean_a

        k = j // 2
        term = mm(hidt[...], G[qb])

        @pl.when(j % 2 == 0)
        def _():
            ups[k] = term.astype(BF)
            up_mate(k).start()

        @pl.when(j % 2 == 1)
        def _():
            upf[...] = term
            up_mate(k).wait_recv()
            total = upf[...] + upr[k].astype(F32)

            @pl.when(k < RING - 1)
            def _():
                uxs[k] = total.astype(BF)
                up_x(k).start()

            @pl.when(k == RING - 1)
            def _():
                accu[...] = total

        return carry

    lax.fori_loop(0, nq, second, 0)

    scale_a = sc[lo_rows]
    coef_a = scale_a * ss[:s]

    def second_backward(q, carry):
        back = mm_nt(bu[...], wd[q]) * gain_ref[q]
        value = G[q, :s].astype(F32) + scale_a * (back - X[q, :s].astype(F32) * coef_a)
        G[q, :s] = value.astype(BF)
        bwd_out(q).start()
        return carry

    lax.fori_loop(0, nq, second_backward, 0)

    for k in range(RING - 1):
        up_x(k).wait_recv()
        accu[...] += uxr[k].astype(F32)
    up_out = pltpu.make_async_copy(accu, gu_h, outs.at[2 * nq])
    up_out.start()
    for k in range(RING - 1):
        down_x(k).wait_recv()
        accd[...] += dxr[k].astype(F32)
    for i in range(1, nq):
        norm_arrival(i).wait_recv()
        but_arrival(i).wait_recv()

    def add_down(q, carry):
        accd[...] += mm(but[q], nall[q])
        return carry

    lax.fori_loop(0, nq, add_down, 0)
    gdo[...] = accd[...].T
    down_out = pltpu.make_async_copy(gdo, gd_h, outs.at[2 * nq + 1])
    down_out.start()

    down.drain()
    up.drain()
    for i in range(7):
        merge_copy(i).wait_send()
    for i in range(1, Z):
        tok_z(i, z).wait_send()
    for i in range(1, n_y):
        tok_y(i, y).wait_send()

    @pl.when(z > 0)
    def _():
        fresh_z(z).wait_send()

    @pl.when((z == 0) & (y > 0))
    def _():
        fresh_y(y).wait_send()

    for i in range(1, nq):
        norm_copy(i).wait_send()
        but_copy(i).wait_send()
    for k in range(RING):
        up_mate(k).wait_send()
        down_mate(k).wait_send()
    for k in range(RING - 1):
        up_x(k).wait_send()
        down_x(k).wait_send()

    def drain(q, carry):
        @pl.when(jnp.logical_not(last))
        def _():
            fwd_send(q).wait_send()

        @pl.when(p > 0)
        def _():
            bwd_send(q).wait_send()

        fwd_out(q).wait()
        bwd_out(q).wait()
        return carry

    lax.fori_loop(0, nq, drain, 0)
    up_out.wait()
    down_out.wait()


def body(
    n_pipe, nq,
    act_in, stash_a, grad_in, text_emb, enc_query, enc_key, enc_value, tok_count, tok_offset,
    merge_gain, w_merge, w_vision, norm_gain, w_down, w_up,
):
    s, width = act_in.shape[2:]
    db, r = w_down.shape[1:]
    enc = enc_query.shape[2]
    heads = enc // HEAD_DIM
    cols = w_vision.shape[1]
    img = enc_key.shape[1]
    n_y = n_pipe // Z
    vm = pltpu.VMEM
    dma = lambda n: pltpu.SemaphoreType.DMA((n,))
    any_spec = pl.BlockSpec(memory_space=pl.ANY)
    vmem_spec = pl.BlockSpec(memory_space=pltpu.VMEM)
    smem_spec = pl.BlockSpec(memory_space=pltpu.SMEM)
    scratch = [
        vm((nq, 2 * s, db), BF),
        vm((nq, 2 * s, db), BF),
        vm((nq, 2 * s, db), BF),
        vm((nq, db, r), BF),
        vm((nq, r, db), BF),
        vm((nq, s, db), BF),
        vm((nq, s, db), BF),
        vm((nq, s, db), BF),
        vm((nq, s, db), BF),
        vm((nq, r, s), BF),
        vm((r, db), F32),
        vm((RING, r, db), BF), vm((RING, r, db), BF), vm((RING, r, db), BF), vm((RING, r, db), BF),
        vm((RING, r, db), BF), vm((RING, r, db), BF), vm((RING, r, db), BF), vm((RING, r, db), BF),
        vm((r, db), F32), vm((r, db), F32),
        vm((nq, r // nq, enc), BF),
        vm((img, enc), BF), vm((img, enc), BF),
        vm((s, cols), BF), vm((r, cols), BF),
        vm((heads * TOK, img), F32),
        vm((TOK, enc), F32),
        vm((n_pipe, 2 * TOK, r), BF),
        vm((s, cols), BF),
        vm((n_y, Z, s, cols), BF),
        vm((2 * s, 1), F32),
        vm((2 * s, r), F32), vm((2 * s, r), F32),
        vm((2 * s, r), BF), vm((r, 2 * s), BF),
        vm((s, r), F32), vm((s, r), BF),
        vm((s, r), F32),
        vm((2 * s, 1), F32),
        vm((s, r), BF),
        vm((db, r), F32),
        dma(8 + 3 * nq),
        dma(8), dma(8), dma(8), dma(8), dma(7), dma(7),
        dma(nq), dma(nq), dma(nq), dma(nq),
        dma(nq), dma(nq), dma(nq), dma(nq),
        dma(RING), dma(RING), dma(RING), dma(RING),
        dma(RING), dma(RING), dma(RING), dma(RING),
        dma(Z), dma(Z), dma(n_y), dma(n_y),
        dma(1), dma(Z), dma(1), dma(n_y),
        dma(2 * nq + 2),
    ]
    fwd, bwd, grad_down, grad_up = pl.pallas_call(
        functools.partial(kernel, n_pipe),
        out_shape=(
            jax.ShapeDtypeStruct((s, width), BF),
            jax.ShapeDtypeStruct((s, width), BF),
            jax.ShapeDtypeStruct((db, r), F32),
            jax.ShapeDtypeStruct((r, db), F32),
        ),
        in_specs=[
            any_spec, any_spec, any_spec, any_spec, any_spec, vmem_spec, any_spec, any_spec,
            smem_spec, smem_spec, vmem_spec, any_spec, vmem_spec, any_spec, any_spec,
        ],
        out_specs=(any_spec,) * 4,
        scratch_shapes=scratch,
        compiler_params=pltpu.CompilerParams(
            collective_id=0, has_side_effects=True, vmem_limit_bytes=56 * 2**20
        ),
        name="relay",
    )(
        act_in[0, 0], stash_a[0, 0], grad_in[0, 0], text_emb[0], w_vision,
        enc_query[0], enc_key[0], enc_value[0], tok_count, tok_offset,
        merge_gain[None], w_merge.T, norm_gain.reshape(nq, 1, db), w_down[0], w_up[0],
    )
    return fwd[None, None], bwd[None, None], grad_down[None], grad_up[None]


def solution(mesh):
    in_specs = (
        P("dp", "pipe", None, None),
        P("dp", "pipe", None, None),
        P("dp", "pipe", None, None),
        P("dp", None, "pipe"),
        P("dp", "pipe", None),
        P("dp", "pipe", None),
        P("dp", "pipe", None),
        P("dp", "pipe"),
        P("dp", "pipe"),
        P(),
        P(None, "dp"),
        P(None, "pipe"),
        P("pipe", None),
        P("pipe", "dp", None),
        P("pipe", None, "dp"),
    )
    out_specs = (
        P("dp", "pipe", None, None),
        P("dp", "pipe", None, None),
        P("pipe", "dp", None),
        P("pipe", None, "dp"),
    )
    step = functools.partial(body, mesh.shape["pipe"], mesh.shape["dp"])
    return jax.shard_map(step, mesh=mesh, in_specs=in_specs, out_specs=out_specs, check_vma=False)
```

time: 319 us -> 147 us (0.46)
  waiting for transfers between devices: 151 us -> 0 us
  Pallas kernels: 0 us -> 137 us
  blocking collectives: 89.9 us -> 0 us
  matrix products: 30.9 us -> 0 us
  between operations: 15.8 us -> 1.94 us
  other arithmetic: 13.4 us -> 0 us
  starting transfers between devices: 6.69 us -> 0 us
    pallas_call x0 -> x1, Pallas kernels: none -> 137 us  [body(): pl.pallas_call(functools.partial(kernel, n_pipe), out_shape=(jax.ShapeDty...]
    ppermute x2 -> x0, waiting for transfers between devices: 89.3 us -> none  [passed_along(): return lax.ppermute(array, axis, pairs)]
    all_gather x2 -> x0, blocking collectives: 77.1 us -> none  [the longest x1 48.1 us: body(): lax.all_gather(attended[None], 'pipe', axis=1, tiled=True)]
    all_gather x4 -> x0, waiting for transfers between devices: 59.3 us -> none  [the longest x1 29.9 us: body(): lax.all_gather(w_up, 'dp', axis=2, tiled=True)]
    dot_general x16 -> x0, matrix products: 30.9 us -> none  [the longest x2 9.4 us: adapter_forward(): jnp.dot(hidden, w_up, preferred_element_type=jnp.float32)]
    unnamed x1 -> x0, blocking collectives: 12.8 us -> none
    convert_element_type x4 -> x0, other arithmetic: 7.69 us -> none  [the longest x2 3.58 us: body(): grad_down, grad_up = (lax.psum_scatter((down0 + down1)[None].astype(jnp.b...]
    ppermute x2 -> x0, starting transfers between devices: 6.27 us -> none  [passed_along(): return lax.ppermute(array, axis, pairs)]
  transfers between devices with their start and end apart: 8 -> 0, of which waited for: 4 -> 0; matrix products, arithmetic and copies ran while one was open for 14% -> 0% of each run, Pallas kernels for 0% -> 0%
where the time goes in v1:
time: 147 us
  Pallas kernels  137 us (93%)
  local copies, waits for them, and re-layouts  7.53 us (5%)
  between operations  1.94 us (1%)
    pallas_call x1, Pallas kernels, body(): pl.pallas_call(functools.partial(kernel, n_pipe), out_shape=(jax.ShapeDty...  137 us
    unnamed x10, local copies, waits for them, and re-layouts  6.21 us

profile of v1, /device:TPU:1, one launch (start us, length us, event | category | flops | bytes accessed | tf_op | source)
XLA Modules:
  0.0 146.6 jit_solution(3334193010746910102)
XLA Ops:
  1.9 1.3 broadcast_in_dim.15.mg_ref
  3.2 137.1 %relay.1 = (bf16[128,8192]{1,0:T(8,128)(2,1)}, bf16[128,8192]{1,0:T(8,128)(2,1)}, f32[1024,128]{1,0:T(8,128)}, f32[128,1024]{1,0:T(8,128)}) custom-call(bf16[128,8192]{1,0:T(8,128)(2,1)} %bitcast.17, bf16[128,8192]{1,0:T(8,128)(2,1)} %bitcast.18, bf16[128,8192]{1,0:T(8,128)(2,1)} %bitcast.19, bf16[128,256]{1,0:T(8,128)(2,1)} %bitcast.27, ...), custom_call_target="tpu_custom_call" | custom-call | tf_op jit(solution)/shard_map/relay/pallas_call | solution.py:718
  140.3 0.0 copy-start
  140.3 3.2 %copy.25 = bf16[1,1,128,8192]{3,2,1,0:T(8,128)(2,1)} copy(bf16[1,1,128,8192]{3,2,1,0:T(8,128)(2,1)} %bitcast.16) | data formatting | bytes 4194304
  143.6 0.0 copy-done
  143.6 0.0 copy-start.2
  143.6 0.0 copy-start.1
  143.6 1.3 copy.26
  144.9 0.1 copy-done.2
  145.0 0.8 copy.27
  145.8 0.0 copy-done.1
  145.8 0.8 copy.28
Async XLA Ops:
  140.3 3.3 %copy-start = (bf16[128,8192]{1,0:T(8,128)(2,1)S(1)}, bf16[128,8192]{1,0:T(8,128)(2,1)}, u32[]{:S(2)}) copy-start(bf16[128,8192]{1,0:T(8,128)(2,1)} %get-tuple-element.9) | copy-start | bytes 6291460
  143.6 1.4 copy-start.2
  143.6 2.2 %copy-start.1 = (f32[128,1024]{1,0:T(8,128)S(1)}, f32[128,1024]{1,0:T(8,128)}, u32[]{:S(2)}) copy-start(f32[128,1024]{1,0:T(8,128)} %get-tuple-element.11) | copy-start | bytes 1572868

commit v2 on v1

--- a/solution.py
+++ b/solution.py
@@ -11,6 +11,7 @@
 EPS = 1e-06
 RING = 4
 Z = 8
+VM = 56
 TOK = 16
 MESH = pl.DeviceIdType.MESH
 BF, F32 = jnp.bfloat16, jnp.float32
@@ -58,10 +59,10 @@
     n_pipe,
     act_h, st_h, gin_h, text_h, wv_h, q_ref, ek_h, ev_h, cnt_ref, off_ref, mg_ref, wm_h, gain_ref, wd_h, wu_h,
     fwd_h, bwd_h, gd_h, gu_h,
-    X, G, N, wd, wu, xin, O0, B0, nall, but, upf, ups, upr, uxs, uxr, dps, dpr, dxs, dxr, accu, accd,
-    wm, ek, ev, text, wv, scr, att, tk, fb, fra, sc, inner, sig, hid, hidt, bh, bu, ic, ss, hid2, gdo,
+    X, G, N, wd, wu, xin, O0, B0, nall, but, ups, upr, uxs, uxr, dps, dpr, dxs, dxr, accu, accd,
+    wm, ek, ev, text, wv, scr, att, tk, fb, fra, rx, ru, rh, rg, rst, rwd, rgn, rb, rp, pk, sc, inner, sig, hid, hidt, bh, bu, bu2, ic, ss, hid2, gdo,
     ld, ags, agr, aus, aur, wms, wmr, zfs, zfr, zbs, zbr, nas, nar, bus, bur,
-    ups_s, ups_r, uxs_s, uxs_r, dps_s, dps_r, dxs_s, dxs_r, tzs, tzr, tys, tyr, fzs, fzr, fys, fyr, outs,
+    ups_s, ups_r, uxs_s, uxs_r, dps_s, dps_r, dxs_s, dxs_r, tzs, tzr, tys, tyr, fzs, fzr, fys, fyr, rfs, rfr, rbs, rbr, outs,
 ):
     nq, s2, db = X.shape
     s = s2 // 2
@@ -212,36 +213,127 @@
         )[i]()
         return rcopy(ref, ref, wms.at[i], wmr.at[i], mate)
 
-    small[0]().wait()
-    down.go(0, 1, 4)
-    small[1]().wait()
+    def tok_z(i, slot_z):
+        ref = tk.at[y * Z + slot_z]
+        return rcopy(ref, ref, tzs.at[i], tzr.at[i], (y * Z + (z + i) % Z, d))
+
+    def tok_y(i, slot_y):
+        ref = tk.at[pl.ds(slot_y * Z, Z)]
+        return rcopy(ref, ref, tys.at[i], tyr.at[i], (((y + i) % n_y) * Z + z, d))
+
+    def fresh_z(slot):
+        return rcopy(fb, fra.at[y, slot], fzs.at[0], fzr.at[slot], (y * Z, d))
+
+    def fresh_y(slot):
+        target = jnp.where(y == n_y - 1, 0, y - 1) * Z
+        return rcopy(fra.at[slot], fra.at[slot], fys.at[slot], fyr.at[slot], (target, d))
+
+    def fwd_send(q):
+        return rcopy(O0.at[q], xin.at[q], zfs.at[q], zfr.at[q], (p + 1, d))
+
+    def bwd_send(q):
+        return rcopy(B0.at[q], G.at[q, pl.ds(0, s)], zbs.at[q], zbr.at[q], (p - 1, d))
+
+    def raw_f(i):
+        src, dst = (
+            lambda: (X.at[d, pl.ds(0, s)], rx),
+            lambda: (wu.at[d], ru),
+            lambda: (hid.at[pl.ds(0, s)], rh),
+        )[i]()
+        return rcopy(src, dst, rfs.at[i], rfr.at[i], (p + 1, d))
+
+    def raw_b(i):
+        src, dst = (
+            lambda: (X.at[d, pl.ds(s, s)], rst),
+            lambda: (G.at[d, pl.ds(s, s)], rg),
+            lambda: (wd.at[d], rwd),
+            lambda: (gain_ref.at[d], rgn),
+            lambda: (bu, rb.at[pl.ds(0, s)]),
+            lambda: (pk, rp),
+            lambda: (hid.at[pl.ds(s, s)], rb.at[pl.ds(s, s)]),
+        )[i]()
+        return rcopy(src, dst, rbs.at[i], rbr.at[i], (p - 1, d))
+
+    def raw_u():
+        return rcopy(wu.at[d], rg, rbs.at[1], rbr.at[1], (p - 1, d))
+
+    inside = jnp.logical_not(last)
+
+    def fwd_block(j):
+        return at((x + pick(j // 2, FWD)) % RING, jnp.where(j % 2 == 0, c, 1 - c))
+
+    def bwd_block(j):
+        return at((x + pick(j // 2, BWD)) % RING, jnp.where(j % 2 == 0, 1 - c, c))
+
+    def down_mate(k):
+        return rcopy(dps.at[k], dpr.at[k], dps_s.at[k], dps_r.at[k], mate)
+
+    def down_x(k):
+        device = (p, at((x + pick(k, BWD)) % RING, c))
+        return rcopy(dxs.at[k], dxr.at[k], dxs_s.at[k], dxs_r.at[k], device)
+
+    def up_mate(k):
+        return rcopy(ups.at[k], upr.at[k], ups_s.at[k], ups_r.at[k], mate)
+
+    def up_x(k):
+        device = (p, at((x + pick(k, BWD)) % RING, c))
+        return rcopy(uxs.at[k], uxr.at[k], uxs_s.at[k], uxs_r.at[k], device)
+
+    def norm_copy(i):
+        target = (d + i) % nq
+        return rcopy(N.at[target, pl.ds(0, s)], nall.at[d], nas.at[i], nar.at[i], (p, target))
+
+    def norm_arrival(i):
+        ref = nall.at[(d + nq - i) % nq]
+        return rcopy(ref, ref, nas.at[i], nar.at[i], mate)
+
+    def but_copy(i):
+        return rcopy(but.at[d], but.at[d], bus.at[i], bur.at[i], (p, (d + i) % nq))
+
+    def but_arrival(i):
+        ref = but.at[(d + nq - i) % nq]
+        return rcopy(ref, ref, bus.at[i], bur.at[i], mate)
+
+    def fwd_out(q):
+        return pltpu.make_async_copy(xin.at[q], cols(fwd_h, q), outs.at[q])
+
+    def bwd_out(q):
+        return pltpu.make_async_copy(G.at[q, pl.ds(0, s)], cols(bwd_h, q), outs.at[nq + q])
+
+    def each(n, step):
+        def run(i, carry):
+            step(i)
+            return carry
+
+        lax.fori_loop(0, n, run, 0, unroll=True)
+
     small[2]().wait()
-
-    ss[...] = jnp.zeros_like(ss)
-
-    def squares(q, carry):
-        for copy in big(q):
-            copy.wait()
-        v = X[q].astype(F32)
-        ss[...] += jnp.sum(v * v, -1, keepdims=True)
-        return carry
-
-    lax.fori_loop(0, nq, squares, 0)
-    sc[...] = lax.rsqrt(ss[...] * (1.0 / width) + EPS)
-
-    def normalise(q, carry):
-        N[q] = (X[q].astype(F32) * sc[...] * gain_ref[q]).astype(BF)
-        return carry
-
-    lax.fori_loop(0, nq, normalise, 0)
-
-    down.wait(0)
-    down.go(2, 5)
-    down.wait(1)
-    down.go(3, 6)
-    up.go(0, 1, 4)
     for i in range(4):
         merge_copy(i).start()
+    small[0]().wait()
+    small[1]().wait()
+    down.go(0, 1, 4)
+    up.go(0, 1, 4)
+
+    for copy in big(d):
+        copy.wait()
+
+    @pl.when(inside)
+    def _():
+        raw_f(0).start()
+        raw_f(1).start()
+
+    @pl.when(p > 0)
+    def _():
+        raw_b(0).start()
+
+    @pl.when((p > 0) & inside)
+    def _():
+        raw_b(1).start()
+
+    @pl.when(last)
+    def _():
+        raw_u().start()
 
     small[3]().wait()
     small[4]().wait()
@@ -257,198 +349,86 @@
         lanes = slice(h * HEAD_DIM, (h + 1) * HEAD_DIM)
         att[:, lanes] = mm(scr[h * TOK:(h + 1) * TOK].astype(BF), ev[:, lanes])
 
-    down.wait(2, 3)
-    down.go(7)
-    down.wait(4, 5, 6, 7)
-
-    inner[...] = jnp.zeros_like(inner)
-
-    def add_inner(q, carry):
-        inner[...] += mm(N[q], wd[q])
+    def wait_big(i, carry):
+        for copy in big((d + i) % nq):
+            copy.wait()
         return carry
 
-    lax.fori_loop(0, nq, add_inner, 0)
-    sig[...] = jax.nn.sigmoid(inner[...])
-    hidden = inner[...] * sig[...]
-    hid[...] = hidden.astype(BF)
-    hidt[...] = hidden.T.astype(BF)
-
-    bh[...] = jnp.zeros_like(bh)
-
-    def fwd_send(q):
-        return rcopy(O0.at[q], xin.at[q], zfs.at[q], zfr.at[q], (p + 1, d))
-
-    def bwd_send(q):
-        return rcopy(B0.at[q], G.at[q, pl.ds(0, s)], zbs.at[q], zbr.at[q], (p - 1, d))
-
-    def fwd_block(j):
-        return at((x + pick(j // 2, FWD)) % RING, jnp.where(j % 2 == 0, c, 1 - c))
-
-    def bwd_block(j):
-        return at((x + pick(j // 2, BWD)) % RING, jnp.where(j % 2 == 0, 1 - c, c))
-
-    def first_forward(j, carry):
-        q = fwd_block(j)
-
-        @pl.when(j == 1)
-        def _():
-            up.wait(4)
-
-        @pl.when(j == 2)
-        def _():
-            up.wait(0)
-            up.go(2, 5)
-            up.wait(1)
-            up.go(3, 6)
-
-        @pl.when(j == 3)
-        def _():
-            up.wait(5)
-
-        @pl.when(j == 5)
-        def _():
-            up.wait(6)
-
-        @pl.when(j == 6)
-        def _():
-            up.wait(2, 3)
-            up.go(7)
-
-        @pl.when(j == 7)
-        def _():
-            up.wait(7)
-
-        out = (X[q, :s].astype(F32) + mm(hid[:s], wu[q])).astype(BF)
-
-        @pl.when(last)
-        def _():
-            G[q, :s] = out
-            G[q, s:] = (X[q, s:].astype(F32) + mm(hid[s:], wu[q])).astype(BF)
-
-        @pl.when(jnp.logical_not(last))
-        def _():
-            O0[q] = out
-            fwd_send(q).start()
-
-        bh[...] += mm_nt(G[q, s:], wu[q])
-        return carry
-
-    lax.fori_loop(0, nq, first_forward, 0)
+    lax.fori_loop(1, nq, wait_big, 0)
+    ss[...] = jnp.zeros_like(ss)
+
+    def squares(q):
+        v = X[q].astype(F32)
+        ss[...] += jnp.sum(v * v, -1, keepdims=True)
+
+    each(nq, squares)
+    sc[...] = lax.rsqrt(ss[...] * (1.0 / width) + EPS)
+
+    def normalise(q):
+        N[q] = (X[q].astype(F32) * sc[...] * gain_ref[q]).astype(BF)
+
+    each(nq, normalise)
 
     for i, k in ((0, 4), (1, 5), (2, 6)):
         merge_arrival(i).wait_recv()
         merge_copy(k).start()
-
-    def factor(rows):
-        sg, inn = sig[rows], inner[rows]
-        value = (bh[...] * sg * (1.0 + inn * (1.0 - sg))).astype(BF)
-        wide = value.astype(F32)
-        return value, wide, jnp.sum(wide * inn, -1, keepdims=True) * (1.0 / width)
-
-    hi_rows, lo_rows = slice(s, 2 * s), slice(0, s)
-
-    bu_b, wide_b, mean_b = factor(hi_rows)
-    bu[...] = bu_b
-    scale_b = sc[hi_rows]
-    coef_b = scale_b * mean_b
-
-    def first_backward(j, carry):
-        q = bwd_block(j)
-        back = mm_nt(bu[...], wd[q]) * gain_ref[q]
-        value = G[q, s:].astype(F32) + scale_b * (back - X[q, s:].astype(F32) * coef_b)
-
-        @pl.when(p > 0)
-        def _():
-            B0[q] = value.astype(BF)
-            bwd_send(q).start()
-
-        return carry
-
-    lax.fori_loop(0, nq, first_backward, 0)
-
     for i in range(3, 7):
         merge_arrival(i).wait_recv()
     rows = att[...].astype(BF).astype(F32)
     scale_m = lax.rsqrt(jnp.mean(rows * rows, -1, keepdims=True) + EPS)
-    rows = (rows * scale_m * mg_ref[...]).astype(BF)
+    rows = (rows * scale_m * mg_ref[...][None, :]).astype(BF)
     tokens = jax.nn.gelu(mm_nt(rows, wm[...].reshape(nq * wm.shape[1], wm.shape[2])))
     tk[p, :TOK] = tokens.astype(BF)
     slot = lax.broadcasted_iota(jnp.int32, (TOK, s), 0)
     place = lax.broadcasted_iota(jnp.int32, (TOK, s), 1)
     live = (slot < cnt_ref[0, 0]) & (place == off_ref[0, 0] + slot)
     tk[p, TOK:] = jnp.where(live, 1.0, 0.0).astype(BF)
-
-    def tok_z(i, slot_z):
-        ref = tk.at[y * Z + slot_z]
-        return rcopy(ref, ref, tzs.at[i], tzr.at[i], (y * Z + (z + i) % Z, d))
-
-    def tok_y(i, slot_y):
-        ref = tk.at[pl.ds(slot_y * Z, Z)]
-        return rcopy(ref, ref, tys.at[i], tyr.at[i], (((y + i) % n_y) * Z + z, d))
-
     for i in range(1, Z):
         tok_z(i, z).start()
 
-    but_b = wide_b.T.astype(BF)
-    bu[...] = but_b
-
-    def down_mate(k):
-        return rcopy(dps.at[k], dpr.at[k], dps_s.at[k], dps_r.at[k], mate)
-
-    def down_x(k):
-        device = (p, at((x + pick(k, BWD)) % RING, c))
-        return rcopy(dxs.at[k], dxr.at[k], dxs_s.at[k], dxs_r.at[k], device)
-
-    def up_mate(k):
-        return rcopy(ups.at[k], upr.at[k], ups_s.at[k], ups_r.at[k], mate)
-
-    def up_x(k):
-        device = (p, at((x + pick(k, BWD)) % RING, c))
-        return rcopy(uxs.at[k], uxr.at[k], uxs_s.at[k], uxs_r.at[k], device)
-
-    def down_first(k, carry):
-        dps[k] = mm(bu[...], N[bwd_block(2 * k), s:]).astype(BF)
-        down_mate(k).start()
-        return carry
-
-    lax.fori_loop(0, RING, down_first, 0)
-
-    def down_second(k, carry):
-        value = mm(bu[...], N[bwd_block(2 * k + 1), s:])
-        down_mate(k).wait_recv()
-        value = value + dpr[k].astype(F32)
-
-        @pl.when(k < RING - 1)
-        def _():
-            dxs[k] = value.astype(BF)
-            down_x(k).start()
-
-        @pl.when(k == RING - 1)
-        def _():
-            accd[...] = value
-
-        return carry
-
-    lax.fori_loop(0, RING, down_second, 0)
-
-    def norm_copy(i):
-        target = (d + i) % nq
-        return rcopy(N.at[target, pl.ds(0, s)], nall.at[d], nas.at[i], nar.at[i], (p, target))
-
-    def norm_arrival(i):
-        ref = nall.at[(d + nq - i) % nq]
-        return rcopy(ref, ref, nas.at[i], nar.at[i], mate)
-
-    for i in range(1, nq):
-        norm_copy(i).start()
-    nall[d] = N[d, :s]
+    @pl.when(p > 0)
+    def _():
+        raw_b(2).start()
+        raw_b(3).start()
+
+    down.wait(0)
+    down.go(2, 5)
+    down.wait(1)
+    down.go(3, 6)
+    up.wait(0)
+    up.go(2, 5)
+    up.wait(1)
+    up.go(3, 6)
 
     for i in range(1, Z):
         tok_z(i, (z + Z - i) % Z).wait_recv()
     for i in range(1, n_y):
         tok_y(i, y).start()
+    down.wait(2, 3)
+    down.go(7)
+    down.wait(4, 5, 6, 7)
+
+    total = mm(N[0], wd[0])
+    for q in range(1, nq):
+        total += mm(N[q], wd[q])
+    inner[...] = total
+    sig[...] = jax.nn.sigmoid(total)
+    hidden = total * sig[...]
+    hid[...] = hidden.astype(BF)
+    hidt[...] = hidden.T.astype(BF)
+
+    @pl.when(inside)
+    def _():
+        raw_f(2).start()
+
+    @pl.when(last)
+    def _():
+        raw_b(6).start()
+
+
     for i in range(1, n_y):
         tok_y(i, (y + n_y - i) % n_y).wait_recv()
+
     small[5]().wait()
     small[6]().wait()
     held = tk[:, :TOK].reshape(n_pipe * TOK, r)
@@ -457,12 +437,6 @@
     marked = mm_tn(spots, jnp.ones_like(held))[:, :1] > 0.5
     fresh = jnp.where(marked, mm(vision, wv[...]), text[...].astype(F32)).astype(BF)
 
-    def fresh_z(slot):
-        return rcopy(fb, fra.at[y, slot], fzs.at[0], fzr.at[slot], (y * Z, d))
-
-    def fresh_y(slot):
-        return rcopy(fra.at[y], fra.at[slot], fys.at[0], fyr.at[slot], (0, d))
-
     @pl.when(z == 0)
     def _():
         fra[y, 0] = fresh
@@ -471,6 +445,91 @@
     def _():
         fb[...] = fresh
         fresh_z(z).start()
+
+    bh[...] = jnp.zeros_like(bh)
+    for k in range(RING):
+        if k == RING - 1:
+            up.wait(2, 3)
+            up.go(7)
+            for i in range(1, nq):
+                norm_copy(i).start()
+            nall[d] = N[d, :s]
+
+            @pl.when(z == 0)
+            def _():
+                for i in range(1, Z):
+                    fresh_z(i).wait_recv()
+
+                @pl.when(y > 0)
+                def _():
+                    fresh_y(y).start()
+
+        up.wait(4 + k)
+        pair = [fwd_block(2 * k), fwd_block(2 * k + 1)]
+        sent = pair[1:] if k == 0 else pair
+        for q in pair:
+            O0[q] = (X[q, :s].astype(F32) + mm(hid[:s], wu[q])).astype(BF)
+
+        @pl.when(last)
+        def _():
+            for q in pair:
+                G[q, :s] = O0[q]
+                G[q, s:] = (X[q, s:].astype(F32) + mm(hid[s:], wu[q])).astype(BF)
+
+        @pl.when(inside)
+        def _():
+            for q in sent:
+                fwd_send(q).start()
+
+        bh[...] += mm_nt(G[pair[0], s:], wu[pair[0]]) + mm_nt(G[pair[1], s:], wu[pair[1]])
+
+    def factor(rows):
+        sg, inn = sig[rows], inner[rows]
+        value = (bh[...] * sg * (1.0 + inn * (1.0 - sg))).astype(BF)
+        wide = value.astype(F32)
+        return value, wide, jnp.sum(wide * inn, -1, keepdims=True) * (1.0 / width)
+
+    hi_rows, lo_rows = slice(s, 2 * s), slice(0, s)
+
+    bu_b, wide_b, mean_b = factor(hi_rows)
+    bu[...] = bu_b
+    scale_b = sc[hi_rows]
+    coef_b = scale_b * mean_b
+    columns = jnp.concatenate([jnp.broadcast_to(scale_b, (s, 8)), jnp.broadcast_to(coef_b, (s, s - 8))], 1).T
+    pk[...] = columns[4:12]
+
+    @pl.when(p > 0)
+    def _():
+        raw_b(4).start()
+        raw_b(5).start()
+
+    for first in range(0, nq - 1, 4):
+        group = [bwd_block(j) for j in range(first, min(first + 4, nq - 1))]
+        for q in group:
+            back = mm_nt(bu[...], wd[q]) * gain_ref[q]
+            value = G[q, s:].astype(F32) + scale_b * (back - X[q, s:].astype(F32) * coef_b)
+            B0[q] = value.astype(BF)
+
+        @pl.when(p > 0)
+        def _():
+            for q in group:
+                bwd_send(q).start()
+
+    turned = wide_b.T.astype(BF)
+    for k in range(RING):
+        dps[k] = mm(turned, N[bwd_block(2 * k), s:]).astype(BF)
+    for k in range(RING):
+        down_mate(k).start()
+    for k in range(RING):
+        down_mate(k).wait_recv()
+    for k in range(RING):
+        value = mm(turned, N[bwd_block(2 * k + 1), s:]) + dpr[k].astype(F32)
+        if k < RING - 1:
+            dxs[k] = value.astype(BF)
+        else:
+            accd[...] = value
+    for k in range(RING - 1):
+        down_x(k).start()
 
     ss[...] = jnp.zeros_like(ss)
     ic[...] = jnp.zeros_like(ic)
@@ -481,65 +540,75 @@
         ss[:s] += jnp.sum(v * v, -1, keepdims=True)
         ic[...] += mm((v * gain_ref[q]).astype(BF), wd[q])
 
-    def fwd_out(q):
-        return pltpu.make_async_copy(xin.at[q], cols(fwd_h, q), outs.at[q])
-
-    def bwd_out(q):
-        return pltpu.make_async_copy(G.at[q, pl.ds(0, s)], cols(bwd_h, q), outs.at[nq + q])
-
-    def but_copy(i):
-        return rcopy(but.at[d], but.at[d], bus.at[i], bur.at[i], (p, (d + i) % nq))
-
-    def but_arrival(i):
-        ref = but.at[(d + nq - i) % nq]
-        return rcopy(ref, ref, bus.at[i], bur.at[i], mate)
-
     def second(j, carry):
-        qf, qb = fwd_block(j), bwd_block(j)
+        qf, qb = fwd_block(j), jnp.where(j == 0, d, bwd_block(j - 1))
+
+        for i in range(2, n_y - 1):
+
+            @pl.when((z == 0) & (j == 2 * i - 3) & (y <= n_y - 1 - i) & (y > 0))
+            def _():
+                fresh_y(y + i - 1).wait_recv()
+                fresh_y(y + i - 1).start()
+
+        @pl.when((p > 0) & (j > 0))
+        def _():
+            fwd_send(qf).wait_recv()
+
+        @pl.when((p > 0) & (j == 0))
+        def _():
+            for i in range(3):
+                raw_f(i).wait_recv()
+            xin[d] = (rx[...].astype(F32) + mm(rh[...], ru[...])).astype(BF)
 
         @pl.when(p > 0)
         def _():
-            fwd_send(qf).wait_recv()
             take_forward(qf)
-
-        @pl.when((j == 1) & (z == 0))
-        def _():
-            for i in range(1, Z):
-                fresh_z(i).wait_recv()
-
-            @pl.when(y > 0)
-            def _():
-                fresh_y(y).start()
 
         @pl.when((j == nq - 1) & (p == 0))
         def _():
             for i in range(1, n_y):
                 fresh_y(i).wait_recv()
 
-            def assemble(q, carry):
+            def assemble(q):
                 for i in range(per):
                     sec = q * per + i
                     xin[q, :, i * dp_cols:(i + 1) * dp_cols] = fra[sec // Z, sec % Z]
                 take_forward(q)
-                return carry
-
-            lax.fori_loop(0, nq, assemble, 0)
+
+            each(nq, assemble)
 
         @pl.when(j == nq - 1)
         def _():
             scale = lax.rsqrt(ss[:s] * (1.0 / width) + EPS)
             hid2[...] = swish(ic[...] * scale).astype(BF)
 
-            def finish(q, carry):
+            def finish(q):
                 xin[q] = (xin[q].astype(F32) + mm(hid2[...], wu[q])).astype(BF)
+
+            each(nq, finish)
+            for q in range(nq):
                 fwd_out(q).start()
-                return carry
-
-            lax.fori_loop(0, nq, finish, 0)
-
-        @pl.when(jnp.logical_not(last))
+
+        @pl.when(inside & (j > 0))
         def _():
             bwd_send(qb).wait_recv()
+
+        @pl.when(inside & (j == 0))
+        def _():
+            for i in range(6):
+                raw_b(i).wait_recv()
+
+        @pl.when((p == n_pipe - 2) & (j == 0))
+        def _():
+            raw_b(6).wait_recv()
+            rg[...] = (rst[...].astype(F32) + mm(rb[s:], rg[...])).astype(BF)
+
+        @pl.when(inside & (j == 0))
+        def _():
+            wide = jnp.concatenate([rp[...], jnp.zeros((s - 8, s), F32)], 0).T
+            back = mm_nt(rb[:s], rwd[...]) * rgn[...]
+            value = rg[...].astype(F32) + wide[:, 0:1] * (back - rst[...].astype(F32) * wide[:, 4:5])
+            G[d, :s] = value.astype(BF)
 
         bh[...] += mm_nt(G[qb, :s], wu[qb])
 
@@ -549,31 +618,26 @@
             but[d] = wide_a.T.astype(BF)
             for i in range(1, nq):
                 but_copy(i).start()
-            bu[...] = bu_a
+            bu2[...] = bu_a
             ss[:s] = mean_a
 
-        k = j // 2
         term = mm(hidt[...], G[qb])
 
-        @pl.when(j % 2 == 0)
-        def _():
-            ups[k] = term.astype(BF)
-            up_mate(k).start()
+        @pl.when(j == 0)
+        def _():
+            accu[...] = term
 
         @pl.when(j % 2 == 1)
         def _():
-            upf[...] = term
+            ups[j // 2] = term.astype(BF)
+            up_mate(j // 2).start()
+
+        @pl.when((j % 2 == 0) & (j > 0))
+        def _():
+            k = j // 2 - 1
             up_mate(k).wait_recv()
-            total = upf[...] + upr[k].astype(F32)
-
-            @pl.when(k < RING - 1)
-            def _():
-                uxs[k] = total.astype(BF)
-                up_x(k).start()
-
-            @pl.when(k == RING - 1)
-            def _():
-                accu[...] = total
+            uxs[k] = (term + upr[k].astype(F32)).astype(BF)
+            up_x(k).start()
 
         return carry
 
@@ -582,33 +646,35 @@
     scale_a = sc[lo_rows]
     coef_a = scale_a * ss[:s]
 
-    def second_backward(q, carry):
-        back = mm_nt(bu[...], wd[q]) * gain_ref[q]
+    def second_backward(q):
+        back = mm_nt(bu2[...], wd[q]) * gain_ref[q]
         value = G[q, :s].astype(F32) + scale_a * (back - X[q, :s].astype(F32) * coef_a)
         G[q, :s] = value.astype(BF)
+
+    each(nq, second_backward)
+    for q in range(nq):
         bwd_out(q).start()
-        return carry
-
-    lax.fori_loop(0, nq, second_backward, 0)
 
     for k in range(RING - 1):
         up_x(k).wait_recv()
-        accu[...] += uxr[k].astype(F32)
+    up_mate(RING - 1).wait_recv()
+    total = accu[...] + upr[RING - 1].astype(F32)
+    for k in range(RING - 1):
+        total += uxr[k].astype(F32)
+    accu[...] = total
     up_out = pltpu.make_async_copy(accu, gu_h, outs.at[2 * nq])
     up_out.start()
     for k in range(RING - 1):
         down_x(k).wait_recv()
-        accd[...] += dxr[k].astype(F32)
     for i in range(1, nq):
         norm_arrival(i).wait_recv()
         but_arrival(i).wait_recv()
-
-    def add_down(q, carry):
-        accd[...] += mm(but[q], nall[q])
-        return carry
-
-    lax.fori_loop(0, nq, add_down, 0)
-    gdo[...] = accd[...].T
+    total = accd[...]
+    for k in range(RING - 1):
+        total += dxr[k].astype(F32)
+    for q in range(nq):
+        total += mm(but[q], nall[q])
+    gdo[...] = total.T
     down_out = pltpu.make_async_copy(gdo, gd_h, outs.at[2 * nq + 1])
     down_out.start()
 
@@ -628,6 +694,11 @@
     @pl.when((z == 0) & (y > 0))
     def _():
         fresh_y(y).wait_send()
+        for i in range(2, n_y - 1):
+
+            @pl.when(y <= n_y - 1 - i)
+            def _():
+                fresh_y(y + i - 1).wait_send()
 
     for i in range(1, nq):
         norm_copy(i).wait_send()
@@ -640,11 +711,11 @@
         down_x(k).wait_send()
 
     def drain(q, carry):
-        @pl.when(jnp.logical_not(last))
+        @pl.when(inside & (q != d))
         def _():
             fwd_send(q).wait_send()
 
-        @pl.when(p > 0)
+        @pl.when((p > 0) & (q != d))
         def _():
             bwd_send(q).wait_send()
 
@@ -653,6 +724,21 @@
         return carry
 
     lax.fori_loop(0, nq, drain, 0)
+
+    @pl.when(inside)
+    def _():
+        for i in range(3):
+            raw_f(i).wait_send()
+
+    @pl.when(p > 0)
+    def _():
+        for i in range(6):
+            raw_b(i).wait_send()
+
+    @pl.when(last)
+    def _():
+        raw_b(6).wait_send()
+
     up_out.wait()
     down_out.wait()
 
@@ -685,7 +771,6 @@
         vm((nq, s, db), BF),
         vm((nq, s, db), BF),
         vm((nq, r, s), BF),
-        vm((r, db), F32),
         vm((RING, r, db), BF), vm((RING, r, db), BF), vm((RING, r, db), BF), vm((RING, r, db), BF),
         vm((RING, r, db), BF), vm((RING, r, db), BF), vm((RING, r, db), BF), vm((RING, r, db), BF),
         vm((r, db), F32), vm((r, db), F32),
@@ -697,10 +782,14 @@
         vm((n_pipe, 2 * TOK, r), BF),
         vm((s, cols), BF),
         vm((n_y, Z, s, cols), BF),
+        vm((s, db), BF), vm((r, db), BF), vm((s, r), BF),
+        vm((s, db), BF), vm((s, db), BF), vm((db, r), BF), vm((1, db), F32),
+        vm((2 * s, r), BF), vm((8, s), F32),
+        vm((8, s), F32),
         vm((2 * s, 1), F32),
         vm((2 * s, r), F32), vm((2 * s, r), F32),
         vm((2 * s, r), BF), vm((r, 2 * s), BF),
-        vm((s, r), F32), vm((s, r), BF),
+        vm((s, r), F32), vm((s, r), BF), vm((s, r), BF),
         vm((s, r), F32),
         vm((2 * s, 1), F32),
         vm((s, r), BF),
@@ -712,7 +801,8 @@
         dma(RING), dma(RING), dma(RING), dma(RING),
         dma(RING), dma(RING), dma(RING), dma(RING),
         dma(Z), dma(Z), dma(n_y), dma(n_y),
-        dma(1), dma(Z), dma(1), dma(n_y),
+        dma(1), dma(Z), dma(n_y), dma(n_y),
+        dma(3), dma(3), dma(7), dma(7),
         dma(2 * nq + 2),
     ]
     fwd, bwd, grad_down, grad_up = pl.pallas_call(
@@ -730,13 +820,13 @@
         out_specs=(any_spec,) * 4,
         scratch_shapes=scratch,
         compiler_params=pltpu.CompilerParams(
-            collective_id=0, has_side_effects=True, vmem_limit_bytes=56 * 2**20
+            collective_id=0, has_side_effects=True, vmem_limit_bytes=VM * 2**20
         ),
         name="relay",
     )(
         act_in[0, 0], stash_a[0, 0], grad_in[0, 0], text_emb[0], w_vision,
         enc_query[0], enc_key[0], enc_value[0], tok_count, tok_offset,
-        merge_gain[None], w_merge.T, norm_gain.reshape(nq, 1, db), w_down[0], w_up[0],
+        merge_gain, w_merge.T, norm_gain.reshape(nq, 1, db), w_down[0], w_up[0],
     )
     return fwd[None, None], bwd[None, None], grad_down[None], grad_up[None]
 

time: 147 us -> 101 us (0.69)
  Pallas kernels: 137 us -> 91.3 us
    pallas_call x1, Pallas kernels: 137 us -> 91.3 us  [body(): pl.pallas_call(functools.partial(kernel, n_pipe), out_shape=(jax.ShapeDty...]
where the time goes in v2:
time: 101 us; the launch traced here: 99.5 us
  Pallas kernels  91.3 us (90%)
  local copies, waits for them, and re-layouts  6.21 us (6%)
  between operations  1.95 us (2%)
    pallas_call x1, Pallas kernels, body(): pl.pallas_call(functools.partial(kernel, n_pipe), out_shape=(jax.ShapeDty...  91.3 us
    unnamed x10, local copies, waits for them, and re-layouts  6.21 us

profile of v2, /device:TPU:1, one launch (start us, length us, event | category | flops | bytes accessed | tf_op | source)
XLA Modules:
  0.0 99.5 jit_solution(8690357325113939331)
XLA Ops:
  1.9 91.3 %relay.1 = (bf16[128,8192]{1,0:T(8,128)(2,1)}, bf16[128,8192]{1,0:T(8,128)(2,1)}, f32[1024,128]{1,0:T(8,128)}, f32[128,1024]{1,0:T(8,128)}) custom-call(bf16[128,8192]{1,0:T(8,128)(2,1)} %bitcast.15, bf16[128,8192]{1,0:T(8,128)(2,1)} %bitcast.16, bf16[128,8192]{1,0:T(8,128)(2,1)} %bitcast.17, bf16[128,256]{1,0:T(8,128)(2,1)} %bitcast.27, ...), custom_call_target="tpu_custom_call" | custom-call | tf_op jit(solution)/shard_map/relay/pallas_call | solution.py:808
  93.2 0.0 copy-start
  93.2 3.2 %copy.25 = bf16[1,1,128,8192]{3,2,1,0:T(8,128)(2,1)} copy(bf16[1,1,128,8192]{3,2,1,0:T(8,128)(2,1)} %bitcast.19) | data formatting | bytes 4194304
  96.5 0.0 copy-done
  96.5 0.0 copy-start.2
  96.5 0.0 copy-start.1
  96.5 1.3 %copy.26 = bf16[1,1,128,8192]{3,2,1,0:T(8,128)(2,1)} copy(bf16[1,1,128,8192]{3,2,1,0:T(8,128)(2,1)S(1)} %bitcast.18) | data formatting | bytes 4194304
  97.8 0.1 copy-done.2
  97.9 0.8 copy.27
  98.7 0.0 copy-done.1
  98.7 0.8 copy.28
Async XLA Ops:
  93.2 3.3 %copy-start = (bf16[128,8192]{1,0:T(8,128)(2,1)S(1)}, bf16[128,8192]{1,0:T(8,128)(2,1)}, u32[]{:S(2)}) copy-start(bf16[128,8192]{1,0:T(8,128)(2,1)} %get-tuple-element.9) | copy-start | bytes 6291460
  96.5 1.4 %copy-start.2 = (f32[1024,128]{1,0:T(8,128)S(1)}, f32[1024,128]{1,0:T(8,128)}, u32[]{:S(2)}) copy-start(f32[1024,128]{1,0:T(8,128)} %get-tuple-element.10) | copy-start | bytes 1572868
  96.5 2.2 %copy-start.1 = (f32[128,1024]{1,0:T(8,128)S(1)}, f32[128,1024]{1,0:T(8,128)}, u32[]{:S(2)}) copy-start(f32[128,1024]{1,0:T(8,128)} %get-tuple-element.11) | copy-start | bytes 1572868

commit v3 on v2

--- a/solution.py
+++ b/solution.py
@@ -53,21 +53,22 @@
 
 FWD = (0, 3, 1, 2)
 BWD = (2, 1, 3, 0)
+FAR = (3, 4, 5)
 
 
 def kernel(
     n_pipe,
     act_h, st_h, gin_h, text_h, wv_h, q_ref, ek_h, ev_h, cnt_ref, off_ref, mg_ref, wm_h, gain_ref, wd_h, wu_h,
     fwd_h, bwd_h, gd_h, gu_h,
-    X, G, N, wd, wu, xin, O0, B0, nall, but, ups, upr, uxs, uxr, dps, dpr, dxs, dxr, accu, accd,
-    wm, ek, ev, text, wv, scr, att, tk, fb, fra, rx, ru, rh, rg, rst, rwd, rgn, rb, rp, pk, sc, inner, sig, hid, hidt, bh, bu, bu2, ic, ss, hid2, gdo,
+    X, G, N, wd, wu, xin, O0, B0, nall, but, ups, upr, uxs, uxr, dps, dpr, dxs, dxr, df, accu, accd,
+    wm, ek, ev, text, wv, scr, att, tk, fra, frw, rx, ru, rh, rg, rst, rwd, rgn, rb, rp, pk, sc, inner, sig, hid, hidt, bh, bu, bu2, ic, ss, hid2, gdo,
     ld, ags, agr, aus, aur, wms, wmr, zfs, zfr, zbs, zbr, nas, nar, bus, bur,
-    ups_s, ups_r, uxs_s, uxs_r, dps_s, dps_r, dxs_s, dxs_r, tzs, tzr, tys, tyr, fzs, fzr, fys, fyr, rfs, rfr, rbs, rbr, outs,
+    ups_s, ups_r, uxs_s, uxs_r, dps_s, dps_r, dxs_s, dxs_r, tzs, tzr, tys, tyr, fzs, fzr, fys, fyr, wzs, wzr, wys, wyr, wxs, wxr, rfs, rfr, rbs, rbr, late, outs,
 ):
     nq, s2, db = X.shape
     s = s2 // 2
     r = wu.shape[1]
-    dp_cols = fb.shape[1]
+    dp_cols = text.shape[1]
     per = db // dp_cols
     n_y = n_pipe // Z
     width = nq * db
@@ -94,10 +95,10 @@
         lambda: load(0, wd_h, wd.at[d]),
         lambda: load(1, wu_h, wu.at[d]),
         lambda: load(2, wm_h, wm.at[d]),
-        lambda: load(3, ek_h, ek),
-        lambda: load(4, ev_h, ev),
-        lambda: load(5, text_h, text),
-        lambda: load(6, wv_h, wv),
+        lambda: load(3, text_h, text),
+        lambda: load(4, wv_h, wv),
+        lambda: load(5, ek_h, ek),
+        lambda: load(6, ev_h, ev),
     ]
 
     def big(q):
@@ -122,25 +123,35 @@
     def greet(device):
         pl.semaphore_signal(barrier, inc=1, device_id=device, device_id_type=MESH)
 
+    up_wrap = (z == Z - 1) & (y < n_y - 1)
+    down_wrap = (z == 0) & (y > 0)
+    inside = p < n_pipe - 1
     for i in range(1, nq):
         greet((p, (d + i) % nq))
-    for i in range(1, Z):
-        greet((y * Z + (z + i) % Z, d))
     for i in range(1, n_y):
         greet((((y + i) % n_y) * Z + z, d))
-    up_wrap = (z == Z - 1) & (y < n_y - 1)
-    down_wrap = (z == 0) & (y > 0)
+
+    @pl.when(inside & jnp.logical_not(up_wrap))
+    def _():
+        greet((p + 1, d))
+
+    @pl.when(p > 0)
+    def _():
+        greet((p - 1, d))
+
+    @pl.when(z == 0)
+    def _():
+        for i in range(2, Z):
+            greet((p + i, d))
+
+    expected = nq - 1 + n_y - 1
+    for condition in (inside, (p > 0) & jnp.logical_not(down_wrap), z >= 2):
+        expected += jnp.where(condition, 1, 0)
+    pl.semaphore_wait(barrier, expected)
 
     @pl.when(up_wrap)
     def _():
-        greet((p + 1, d))
-
-    @pl.when(down_wrap)
-    def _():
-        greet((p - 1, d))
-
-    extra = jnp.where(up_wrap | down_wrap, 1, 0)
-    pl.semaphore_wait(barrier, nq - 1 + Z - 1 + n_y - 1 + extra)
+        pl.semaphore_signal(late, inc=1, device_id=(p + 1, d), device_id_type=MESH)
 
     class Gather:
         def __init__(self, buf, send, recv):
@@ -213,20 +224,36 @@
         )[i]()
         return rcopy(ref, ref, wms.at[i], wmr.at[i], mate)
 
-    def tok_z(i, slot_z):
-        ref = tk.at[y * Z + slot_z]
-        return rcopy(ref, ref, tzs.at[i], tzr.at[i], (y * Z + (z + i) % Z, d))
-
-    def tok_y(i, slot_y):
-        ref = tk.at[pl.ds(slot_y * Z, Z)]
-        return rcopy(ref, ref, tys.at[i], tyr.at[i], (((y + i) % n_y) * Z + z, d))
-
-    def fresh_z(slot):
-        return rcopy(fb, fra.at[y, slot], fzs.at[0], fzr.at[slot], (y * Z, d))
-
-    def fresh_y(slot):
+    def to_row(src, dst, send, recv, slot_z):
+        return rcopy(src, dst, send.at[0], recv.at[slot_z], (y * Z, d))
+
+    def text_z(slot):
+        return to_row(text, fra.at[y, slot], fzs, fzr, slot)
+
+    def map_z(slot):
+        return to_row(wv, frw.at[c, y, slot // 2], wzs, wzr, slot)
+
+    def tok_z(slot):
+        ref = tk.at[y * Z + slot]
+        return to_row(ref, ref, tzs, tzr, slot)
+
+    def to_first(ref, send, recv, slot_y):
         target = jnp.where(y == n_y - 1, 0, y - 1) * Z
-        return rcopy(fra.at[slot], fra.at[slot], fys.at[slot], fyr.at[slot], (target, d))
+        return rcopy(ref, ref, send.at[slot_y], recv.at[slot_y], (target, d))
+
+    def text_y(slot):
+        return to_first(fra.at[slot], fys, fyr, slot)
+
+    def map_y(slot):
+        return to_first(frw.at[c, slot], wys, wyr, slot)
+
+    def tok_y(slot):
+        return to_first(tk.at[pl.ds(slot * Z, Z)], tys, tyr, slot)
+
+    def map_mate(half):
+        return rcopy(frw.at[c], frw.at[half], wxs.at[0], wxr.at[0], mate)
+
+    mine = z % 2 == c
 
     def fwd_send(q):
         return rcopy(O0.at[q], xin.at[q], zfs.at[q], zfr.at[q], (p + 1, d))
@@ -257,8 +284,6 @@
     def raw_u():
         return rcopy(wu.at[d], rg, rbs.at[1], rbr.at[1], (p - 1, d))
 
-    inside = jnp.logical_not(last)
-
     def fwd_block(j):
         return at((x + pick(j // 2, FWD)) % RING, jnp.where(j % 2 == 0, c, 1 - c))
 
@@ -268,16 +293,32 @@
     def down_mate(k):
         return rcopy(dps.at[k], dpr.at[k], dps_s.at[k], dps_r.at[k], mate)
 
-    def down_x(k):
-        device = (p, at((x + pick(k, BWD)) % RING, c))
-        return rcopy(dxs.at[k], dxr.at[k], dxs_s.at[k], dxs_r.at[k], device)
+    def along_x(src, dst, send, recv, i):
+        ref, device = (
+            (lambda v: v.at[0, pl.ds(0, r // 2)], left),
+            (lambda v: v.at[1], right),
+            (lambda v: v.at[2], left),
+            (lambda v: v.at[0, pl.ds(r // 2, r // 2)], right),
+        )[i]
+        return rcopy(ref(src), ref(dst), send.at[i], recv.at[i], device)
+
+    def down_x(i):
+        return along_x(dxs, dxr, dxs_s, dxs_r, i)
+
+    def near(src, half, k, total):
+        lo, hi = total[:r // 2], total[r // 2:]
+        if k == 1:
+            hi = hi + half[0, r // 2:].astype(F32)
+        else:
+            lo = lo + half[0, :r // 2].astype(F32)
+        src[k, :r // 2] = lo.astype(BF)
+        src[k, r // 2:] = hi.astype(BF)
 
     def up_mate(k):
         return rcopy(ups.at[k], upr.at[k], ups_s.at[k], ups_r.at[k], mate)
 
-    def up_x(k):
-        device = (p, at((x + pick(k, BWD)) % RING, c))
-        return rcopy(uxs.at[k], uxr.at[k], uxs_s.at[k], uxs_r.at[k], device)
+    def up_x(i):
+        return along_x(uxs, uxr, uxs_s, uxs_r, i)
 
     def norm_copy(i):
         target = (d + i) % nq
@@ -307,13 +348,32 @@
 
         lax.fori_loop(0, n, run, 0, unroll=True)
 
-    small[2]().wait()
-    for i in range(4):
-        merge_copy(i).start()
     small[0]().wait()
     small[1]().wait()
     down.go(0, 1, 4)
     up.go(0, 1, 4)
+    small[2]().wait()
+    for i in range(4):
+        merge_copy(i).start()
+
+    small[3]().wait()
+    small[4]().wait()
+
+    @pl.when(z > 0)
+    def _():
+        text_z(z).start()
+
+    @pl.when((z > 0) & mine)
+    def _():
+        map_z(z).start()
+
+    @pl.when(z == 0)
+    def _():
+        fra[y, 0] = text[...]
+
+    @pl.when((z == 0) & mine)
+    def _():
+        frw[0, y, 0] = wv[...]
 
     for copy in big(d):
         copy.wait()
@@ -323,11 +383,11 @@
         raw_f(0).start()
         raw_f(1).start()
 
-    @pl.when(p > 0)
+    @pl.when((p > 0) & jnp.logical_not(down_wrap))
     def _():
         raw_b(0).start()
 
-    @pl.when((p > 0) & inside)
+    @pl.when((p > 0) & inside & jnp.logical_not(down_wrap))
     def _():
         raw_b(1).start()
 
@@ -335,8 +395,8 @@
     def _():
         raw_u().start()
 
-    small[3]().wait()
-    small[4]().wait()
+    small[5]().wait()
+    small[6]().wait()
     query = jnp.concatenate([q_ref[...].astype(F32), jnp.zeros((TOK - q_ref.shape[0], q_ref.shape[1]), F32)], 0)
     query = query.astype(BF)
     for h in range(heads):
@@ -369,27 +429,11 @@
 
     each(nq, normalise)
 
-    for i, k in ((0, 4), (1, 5), (2, 6)):
-        merge_arrival(i).wait_recv()
-        merge_copy(k).start()
-    for i in range(3, 7):
-        merge_arrival(i).wait_recv()
-    rows = att[...].astype(BF).astype(F32)
-    scale_m = lax.rsqrt(jnp.mean(rows * rows, -1, keepdims=True) + EPS)
-    rows = (rows * scale_m * mg_ref[...][None, :]).astype(BF)
-    tokens = jax.nn.gelu(mm_nt(rows, wm[...].reshape(nq * wm.shape[1], wm.shape[2])))
-    tk[p, :TOK] = tokens.astype(BF)
-    slot = lax.broadcasted_iota(jnp.int32, (TOK, s), 0)
-    place = lax.broadcasted_iota(jnp.int32, (TOK, s), 1)
-    live = (slot < cnt_ref[0, 0]) & (place == off_ref[0, 0] + slot)
-    tk[p, TOK:] = jnp.where(live, 1.0, 0.0).astype(BF)
-    for i in range(1, Z):
-        tok_z(i, z).start()
-
-    @pl.when(p > 0)
-    def _():
-        raw_b(2).start()
-        raw_b(3).start()
+    @pl.when(down_wrap)
+    def _():
+        pl.semaphore_wait(late, 1)
+        raw_b(0).start()
+        raw_b(1).start()
 
     down.wait(0)
     down.go(2, 5)
@@ -399,19 +443,69 @@
     up.go(2, 5)
     up.wait(1)
     up.go(3, 6)
-
-    for i in range(1, Z):
-        tok_z(i, (z + Z - i) % Z).wait_recv()
-    for i in range(1, n_y):
-        tok_y(i, y).start()
+    for i, k in ((0, 4), (1, 5), (2, 6)):
+        merge_arrival(i).wait_recv()
+        merge_copy(k).start()
+    @pl.when(p > 0)
+    def _():
+        raw_b(2).start()
+        raw_b(3).start()
+
+    @pl.when(z == 0)
+    def _():
+        for i in range(1, Z):
+            text_z(i).wait_recv()
+
+            @pl.when(i % 2 == c)
+            def _():
+                map_z(i).wait_recv()
+
+        @pl.when(y > 0)
+        def _():
+            text_y(y).start()
+            map_y(y).start()
+
+    order = [fwd_block(j) for j in range(nq)]
+
+    def inner_of(blocks):
+        for q in blocks:
+            inner[...] += mm(N[q], wd[q])
+
+    def back_of(blocks):
+        for q in blocks:
+            bh[...] += mm_nt(G[q, s:], wu[q])
+
+    inner[...] = jnp.zeros_like(inner)
+    bh[...] = jnp.zeros_like(bh)
+    down.wait(4, 5, 6)
+    inner_of(order[:6])
+    up.wait(4, 5, 6)
+
+    @pl.when(inside)
+    def _():
+        back_of(order[:6])
+
+    for i in range(3, 7):
+        merge_arrival(i).wait_recv()
+    rows = att[...].astype(BF).astype(F32)
+    scale_m = lax.rsqrt(jnp.mean(rows * rows, -1, keepdims=True) + EPS)
+    rows = (rows * scale_m * mg_ref[...][None, :]).astype(BF)
+    tokens = mm_nt(rows, wm[...].reshape(nq * wm.shape[1], wm.shape[2]))
+    tk[p, :TOK] = jax.nn.gelu(tokens).astype(BF)
+    slot = lax.broadcasted_iota(jnp.int32, (TOK, s), 0)
+    place = lax.broadcasted_iota(jnp.int32, (TOK, s), 1)
+    live = (slot < cnt_ref[0, 0]) & (place == off_ref[0, 0] + slot)
+    tk[p, TOK:] = jnp.where(live, 1.0, 0.0).astype(BF)
+    @pl.when(z > 0)
+    def _():
+        tok_z(z).start()
+
     down.wait(2, 3)
     down.go(7)
-    down.wait(4, 5, 6, 7)
-
-    total = mm(N[0], wd[0])
-    for q in range(1, nq):
-        total += mm(N[q], wd[q])
-    inner[...] = total
+    inner_of(order[6:7])
+    down.wait(7)
+    inner_of(order[7:])
+    total = inner[...]
     sig[...] = jax.nn.sigmoid(total)
     hidden = total * sig[...]
     hid[...] = hidden.astype(BF)
@@ -426,62 +520,43 @@
         raw_b(6).start()
 
 
-    for i in range(1, n_y):
-        tok_y(i, (y + n_y - i) % n_y).wait_recv()
-
-    small[5]().wait()
-    small[6]().wait()
-    held = tk[:, :TOK].reshape(n_pipe * TOK, r)
-    spots = tk[:, TOK:].reshape(n_pipe * TOK, s)
-    vision = mm_tn(spots, held).astype(BF)
-    marked = mm_tn(spots, jnp.ones_like(held))[:, :1] > 0.5
-    fresh = jnp.where(marked, mm(vision, wv[...]), text[...].astype(F32)).astype(BF)
-
-    @pl.when(z == 0)
-    def _():
-        fra[y, 0] = fresh
-
-    @pl.when(z > 0)
-    def _():
-        fb[...] = fresh
-        fresh_z(z).start()
-
-    bh[...] = jnp.zeros_like(bh)
-    for k in range(RING):
-        if k == RING - 1:
-            up.wait(2, 3)
-            up.go(7)
-            for i in range(1, nq):
-                norm_copy(i).start()
-            nall[d] = N[d, :s]
-
-            @pl.when(z == 0)
-            def _():
-                for i in range(1, Z):
-                    fresh_z(i).wait_recv()
-
-                @pl.when(y > 0)
-                def _():
-                    fresh_y(y).start()
-
-        up.wait(4 + k)
-        pair = [fwd_block(2 * k), fwd_block(2 * k + 1)]
-        sent = pair[1:] if k == 0 else pair
-        for q in pair:
+    def leave(blocks):
+        for q in blocks:
             O0[q] = (X[q, :s].astype(F32) + mm(hid[:s], wu[q])).astype(BF)
 
+        @pl.when(inside)
+        def _():
+            for q in blocks:
+                if q is not order[0]:
+                    fwd_send(q).start()
+
         @pl.when(last)
         def _():
-            for q in pair:
+            for q in blocks:
                 G[q, :s] = O0[q]
                 G[q, s:] = (X[q, s:].astype(F32) + mm(hid[s:], wu[q])).astype(BF)
-
-        @pl.when(inside)
-        def _():
-            for q in sent:
-                fwd_send(q).start()
-
-        bh[...] += mm_nt(G[pair[0], s:], wu[pair[0]]) + mm_nt(G[pair[1], s:], wu[pair[1]])
+            back_of(blocks)
+
+    leave(order[:4])
+    up.wait(2, 3)
+    up.go(7)
+    for i in range(1, nq):
+        if i not in FAR:
+            norm_copy(i).start()
+    leave(order[4:6])
+
+    @pl.when(inside)
+    def _():
+        back_of(order[6:7])
+
+    up.wait(7)
+
+    @pl.when(inside)
+    def _():
+        back_of(order[7:])
+
+    leave(order[6:])
+    nall[d] = N[d, :s]
 
     def factor(rows):
         sg, inn = sig[rows], inner[rows]
@@ -524,12 +599,33 @@
         down_mate(k).wait_recv()
     for k in range(RING):
         value = mm(turned, N[bwd_block(2 * k + 1), s:]) + dpr[k].astype(F32)
-        if k < RING - 1:
-            dxs[k] = value.astype(BF)
+        if k == 0:
+            dxs[0] = value.astype(BF)
+            down_x(0).start()
+            down_x(3).start()
+        elif k < RING - 1:
+            df[k - 1] = value
         else:
             accd[...] = value
-    for k in range(RING - 1):
-        down_x(k).start()
+    for i in FAR:
+        norm_copy(i).start()
+
+    @pl.when(z == 0)
+    def _():
+        for i in range(1, Z):
+            tok_z(i).wait_recv()
+
+        @pl.when(y > 0)
+        def _():
+            tok_y(y).start()
+
+        for i in range(2, n_y - 1):
+
+            @pl.when((y <= n_y - 1 - i) & (y > 0))
+            def _():
+                for relay in (text_y, map_y):
+                    relay(y + i - 1).wait_recv()
+                    relay(y + i - 1).start()
 
     ss[...] = jnp.zeros_like(ss)
     ic[...] = jnp.zeros_like(ic)
@@ -547,8 +643,8 @@
 
             @pl.when((z == 0) & (j == 2 * i - 3) & (y <= n_y - 1 - i) & (y > 0))
             def _():
-                fresh_y(y + i - 1).wait_recv()
-                fresh_y(y + i - 1).start()
+                tok_y(y + i - 1).wait_recv()
+                tok_y(y + i - 1).start()
 
         @pl.when((p > 0) & (j > 0))
         def _():
@@ -564,15 +660,29 @@
         def _():
             take_forward(qf)
 
-        @pl.when((j == nq - 1) & (p == 0))
+        @pl.when((j == 4) & (p == 0))
         def _():
             for i in range(1, n_y):
-                fresh_y(i).wait_recv()
+                map_y(i).wait_recv()
+            map_mate(c).start()
+
+        @pl.when((j == nq - 2) & (p == 0))
+        def _():
+            for i in range(1, n_y):
+                text_y(i).wait_recv()
+                tok_y(i).wait_recv()
+            map_mate(1 - c).wait_recv()
+            held = tk[:, :TOK].reshape(n_pipe * TOK, r)
+            spots = tk[:, TOK:].reshape(n_pipe * TOK, s)
+            vision = mm_tn(spots, held).astype(BF)
+            marked = mm_tn(spots, jnp.ones_like(held))[:, :1] > 0.5
 
             def assemble(q):
                 for i in range(per):
                     sec = q * per + i
-                    xin[q, :, i * dp_cols:(i + 1) * dp_cols] = fra[sec // Z, sec % Z]
+                    mapped = mm(vision, frw[sec % 2, sec // Z, sec % Z // 2])
+                    words = fra[sec // Z, sec % Z].astype(F32)
+                    xin[q, :, i * dp_cols:(i + 1) * dp_cols] = jnp.where(marked, mapped, words).astype(BF)
                 take_forward(q)
 
             each(nq, assemble)
@@ -632,12 +742,28 @@
             ups[j // 2] = term.astype(BF)
             up_mate(j // 2).start()
 
-        @pl.when((j % 2 == 0) & (j > 0))
-        def _():
-            k = j // 2 - 1
-            up_mate(k).wait_recv()
-            uxs[k] = (term + upr[k].astype(F32)).astype(BF)
-            up_x(k).start()
+        @pl.when(j == 2)
+        def _():
+            up_mate(0).wait_recv()
+            uxs[0] = (term + upr[0].astype(F32)).astype(BF)
+            up_x(0).start()
+            up_x(3).start()
+
+        for k, part in ((1, 3), (2, 0)):
+
+            @pl.when(j == 2 * k + 2)
+            def _():
+                up_mate(k).wait_recv()
+                up_x(part).wait_recv()
+                near(uxs, uxr, k, term + upr[k].astype(F32))
+                up_x(k).start()
+
+        @pl.when(j == 1)
+        def _():
+            for k, part in ((1, 3), (2, 0)):
+                down_x(part).wait_recv()
+                near(dxs, dxr, k, df[k - 1])
+                down_x(k).start()
 
         return carry
 
@@ -655,22 +781,22 @@
     for q in range(nq):
         bwd_out(q).start()
 
-    for k in range(RING - 1):
+    for k in (1, 2):
         up_x(k).wait_recv()
     up_mate(RING - 1).wait_recv()
     total = accu[...] + upr[RING - 1].astype(F32)
-    for k in range(RING - 1):
+    for k in (1, 2):
         total += uxr[k].astype(F32)
     accu[...] = total
     up_out = pltpu.make_async_copy(accu, gu_h, outs.at[2 * nq])
     up_out.start()
-    for k in range(RING - 1):
+    for k in (1, 2):
         down_x(k).wait_recv()
     for i in range(1, nq):
         norm_arrival(i).wait_recv()
         but_arrival(i).wait_recv()
     total = accd[...]
-    for k in range(RING - 1):
+    for k in (1, 2):
         total += dxr[k].astype(F32)
     for q in range(nq):
         total += mm(but[q], nall[q])
@@ -682,23 +808,28 @@
     up.drain()
     for i in range(7):
         merge_copy(i).wait_send()
-    for i in range(1, Z):
-        tok_z(i, z).wait_send()
-    for i in range(1, n_y):
-        tok_y(i, y).wait_send()
-
     @pl.when(z > 0)
     def _():
-        fresh_z(z).wait_send()
+        text_z(z).wait_send()
+        tok_z(z).wait_send()
+
+    @pl.when((z > 0) & mine)
+    def _():
+        map_z(z).wait_send()
 
     @pl.when((z == 0) & (y > 0))
     def _():
-        fresh_y(y).wait_send()
-        for i in range(2, n_y - 1):
-
-            @pl.when(y <= n_y - 1 - i)
-            def _():
-                fresh_y(y + i - 1).wait_send()
+        for relay in (text_y, map_y, tok_y):
+            relay(y).wait_send()
+            for i in range(2, n_y - 1):
+
+                @pl.when(y <= n_y - 1 - i)
+                def _():
+                    relay(y + i - 1).wait_send()
+
+    @pl.when(p == 0)
+    def _():
+        map_mate(c).wait_send()
 
     for i in range(1, nq):
         norm_copy(i).wait_send()
@@ -706,9 +837,9 @@
     for k in range(RING):
         up_mate(k).wait_send()
         down_mate(k).wait_send()
-    for k in range(RING - 1):
-        up_x(k).wait_send()
-        down_x(k).wait_send()
+    for i in range(RING):
+        up_x(i).wait_send()
+        down_x(i).wait_send()
 
     def drain(q, carry):
         @pl.when(inside & (q != d))
@@ -741,6 +872,30 @@
 
     up_out.wait()
     down_out.wait()
+
+
+PIECES = 4
+
+
+def hand_over(*refs):
+    held, sems = refs[8:12], refs[12]
+    loads, stores = [], []
+    for i in range(4):
+        src, dst = refs[i], refs[4 + i]
+        dst = dst.at[0, 0] if len(dst.shape) == 4 else dst.at[0]
+        rows = src.shape[0] // PIECES
+        for k in range(PIECES):
+            part = pl.ds(k * rows, rows)
+            n = 2 * (i * PIECES + k)
+            loads.append(pltpu.make_async_copy(src.at[part], held[i].at[part], sems.at[n]))
+            stores.append(pltpu.make_async_copy(held[i].at[part], dst.at[part], sems.at[n + 1]))
+    for copy in loads:
+        copy.start()
+    for load, store in zip(loads, stores):
+        load.wait()
+        store.start()
+    for copy in stores:
+        copy.wait()
 
 
 def body(
@@ -758,6 +913,7 @@
     vm = pltpu.VMEM
     dma = lambda n: pltpu.SemaphoreType.DMA((n,))
     any_spec = pl.BlockSpec(memory_space=pl.ANY)
+    hbm_spec = pl.BlockSpec(memory_space=pltpu.HBM)
     vmem_spec = pl.BlockSpec(memory_space=pltpu.VMEM)
     smem_spec = pl.BlockSpec(memory_space=pltpu.SMEM)
     scratch = [
@@ -773,6 +929,7 @@
         vm((nq, r, s), BF),
         vm((RING, r, db), BF), vm((RING, r, db), BF), vm((RING, r, db), BF), vm((RING, r, db), BF),
         vm((RING, r, db), BF), vm((RING, r, db), BF), vm((RING, r, db), BF), vm((RING, r, db), BF),
+        vm((2, r, db), F32),
         vm((r, db), F32), vm((r, db), F32),
         vm((nq, r // nq, enc), BF),
         vm((img, enc), BF), vm((img, enc), BF),
@@ -780,8 +937,8 @@
         vm((heads * TOK, img), F32),
         vm((TOK, enc), F32),
         vm((n_pipe, 2 * TOK, r), BF),
-        vm((s, cols), BF),
         vm((n_y, Z, s, cols), BF),
+        vm((2, n_y, Z // 2, r, cols), BF),
         vm((s, db), BF), vm((r, db), BF), vm((s, r), BF),
         vm((s, db), BF), vm((s, db), BF), vm((db, r), BF), vm((1, db), F32),
         vm((2 * s, r), BF), vm((8, s), F32),
@@ -800,9 +957,11 @@
         dma(nq), dma(nq), dma(nq), dma(nq),
         dma(RING), dma(RING), dma(RING), dma(RING),
         dma(RING), dma(RING), dma(RING), dma(RING),
-        dma(Z), dma(Z), dma(n_y), dma(n_y),
         dma(1), dma(Z), dma(n_y), dma(n_y),
+        dma(1), dma(Z), dma(n_y), dma(n_y),
+        dma(1), dma(Z), dma(n_y), dma(n_y), dma(1), dma(1),
         dma(3), dma(3), dma(7), dma(7),
+        pltpu.SemaphoreType.REGULAR,
         dma(2 * nq + 2),
     ]
     fwd, bwd, grad_down, grad_up = pl.pallas_call(
@@ -814,8 +973,8 @@
             jax.ShapeDtypeStruct((r, db), F32),
         ),
         in_specs=[
-            any_spec, any_spec, any_spec, any_spec, any_spec, vmem_spec, any_spec, any_spec,
-            smem_spec, smem_spec, vmem_spec, any_spec, vmem_spec, any_spec, any_spec,
+            hbm_spec, hbm_spec, hbm_spec, hbm_spec, hbm_spec, vmem_spec, hbm_spec, hbm_spec,
+            smem_spec, smem_spec, vmem_spec, hbm_spec, vmem_spec, hbm_spec, hbm_spec,
         ],
         out_specs=(any_spec,) * 4,
         scratch_shapes=scratch,
@@ -828,7 +987,21 @@
         enc_query[0], enc_key[0], enc_value[0], tok_count, tok_offset,
         merge_gain, w_merge.T, norm_gain.reshape(nq, 1, db), w_down[0], w_up[0],
     )
-    return fwd[None, None], bwd[None, None], grad_down[None], grad_up[None]
+    done = pl.pallas_call(
+        hand_over,
+        out_shape=(
+            jax.ShapeDtypeStruct((1, 1, s, width), BF),
+            jax.ShapeDtypeStruct((1, 1, s, width), BF),
+            jax.ShapeDtypeStruct((1, db, r), F32),
+            jax.ShapeDtypeStruct((1, r, db), F32),
+        ),
+        in_specs=[any_spec] * 4,
+        out_specs=(any_spec,) * 4,
+        scratch_shapes=[vm((s, width), BF), vm((s, width), BF), vm((db, r), F32), vm((r, db), F32), dma(8 * PIECES)],
+        compiler_params=pltpu.CompilerParams(vmem_limit_bytes=VM * 2**20),
+        name="hand_over",
+    )(fwd, bwd, grad_down, grad_up)
+    return done
 
 
 def solution(mesh):

time: 101 us -> 92.5 us (0.916)
  local copies, waits for them, and re-layouts: 6.21 us -> 0 us
  Pallas kernels: 91.3 us -> 88.6 us
    pallas_call x1, Pallas kernels: 91.3 us -> 84 us  [body(): pl.pallas_call(functools.partial(kernel, n_pipe), out_shape=(jax.ShapeDty...]
    unnamed x10 -> x0, local copies, waits for them, and re-layouts: 6.21 us -> none
    pallas_call x0 -> x1, Pallas kernels: none -> 4.66 us  [body(): pl.pallas_call(hand_over, out_shape=(jax.ShapeDtypeStruct((1, 1, s, width...]
where the time goes in v3:
time: 92.5 us; the launch traced here: 90.7 us
  Pallas kernels  88.6 us (96%)
  between operations  2.1 us (2%)
    pallas_call x1, Pallas kernels, body(): pl.pallas_call(functools.partial(kernel, n_pipe), out_shape=(jax.ShapeDty...  84 us
    pallas_call x1, Pallas kernels, body(): pl.pallas_call(hand_over, out_shape=(jax.ShapeDtypeStruct((1, 1, s, width...  4.66 us

profile of v3, /device:TPU:1, one launch (start us, length us, event | category | flops | bytes accessed | tf_op | source)
XLA Modules:
  0.0 90.7 jit_solution(7159832054506628821)
XLA Ops:
  1.9 84.0 %relay.1 = (bf16[128,8192]{1,0:T(8,128)(2,1)}, bf16[128,8192]{1,0:T(8,128)(2,1)}, f32[1024,128]{1,0:T(8,128)}, f32[128,1024]{1,0:T(8,128)}) custom-call(bf16[128,8192]{1,0:T(8,128)(2,1)} %bitcast.11, bf16[128,8192]{1,0:T(8,128)(2,1)} %bitcast.12, bf16[128,8192]{1,0:T(8,128)(2,1)} %bitcast.13, bf16[128,256]{1,0:T(8,128)(2,1)} %bitcast.19, ...), custom_call_target="tpu_custom_call" | custom-call | tf_op jit(solution)/shard_map/relay/pallas_call | solution.py:967
  85.9 4.7 %hand_over.1 = (bf16[1,1,128,8192]{3,2,1,0:T(8,128)(2,1)}, bf16[1,1,128,8192]{3,2,1,0:T(8,128)(2,1)}, f32[1,1024,128]{2,1,0:T(8,128)}, f32[1,128,1024]{2,1,0:T(8,128)}) custom-call(bf16[128,8192]{1,0:T(8,128)(2,1)} %get-tuple-element.8.refs_0_, bf16[128,8192]{1,0:T(8,128)(2,1)} %get-tuple-element.9.refs_1_, f32[1024,128]{1,0:T(8,128)} %get-tuple-element.10.refs_2_, ...), custom_call_target="tpu_custom_call" | custom-call | tf_op jit(solution)/shard_map/hand_over/pallas_call | solution.py:990

commit v4 on v3

--- a/solution.py
+++ b/solution.py
@@ -161,28 +161,32 @@
         def copy(self, i):
             lo, hi = pl.ds(0, self.half), pl.ds(self.half, self.half)
             ref, device = (
-                lambda: (self.buf.at[d], right),
-                lambda: (self.buf.at[d], left),
+                lambda: (self.buf.at[d, lo], right),
+                lambda: (self.buf.at[d, hi], left),
                 lambda: (self.buf.at[at(xl, c), lo], right),
                 lambda: (self.buf.at[at(xr, c), hi], left),
                 lambda: (self.buf.at[d], mate),
                 lambda: (self.buf.at[at(xl, c)], mate),
                 lambda: (self.buf.at[at(xr, c)], mate),
                 lambda: (self.buf.at[at(xo, c)], mate),
+                lambda: (self.buf.at[d, hi], right),
+                lambda: (self.buf.at[d, lo], left),
             )[i]()
             return rcopy(ref, ref, self.send.at[i], self.recv.at[i], device)
 
         def arrival(self, i):
             lo, hi = pl.ds(0, self.half), pl.ds(self.half, self.half)
             ref = (
-                lambda: self.buf.at[at(xl, c)],
-                lambda: self.buf.at[at(xr, c)],
+                lambda: self.buf.at[at(xl, c), lo],
+                lambda: self.buf.at[at(xr, c), hi],
                 lambda: self.buf.at[at(xo, c), lo],
                 lambda: self.buf.at[at(xo, c), hi],
                 lambda: self.buf.at[at(x, 1 - c)],
                 lambda: self.buf.at[at(xl, 1 - c)],
                 lambda: self.buf.at[at(xr, 1 - c)],
                 lambda: self.buf.at[at(xo, 1 - c)],
+                lambda: self.buf.at[at(xl, c), hi],
+                lambda: self.buf.at[at(xr, c), lo],
             )[i]()
             return rcopy(ref, ref, self.send.at[i], self.recv.at[i], mate)
 
@@ -195,7 +199,7 @@
                 self.arrival(i).wait_recv()
 
         def drain(self):
-            for i in range(8):
+            for i in range(10):
                 self.copy(i).wait_send()
 
     down, up = Gather(wd, ags, agr), Gather(wu, aus, aur)
@@ -350,8 +354,8 @@
 
     small[0]().wait()
     small[1]().wait()
-    down.go(0, 1, 4)
-    up.go(0, 1, 4)
+    down.go(0, 1, 8, 9, 4)
+    up.go(0, 1, 8, 9, 4)
     small[2]().wait()
     for i in range(4):
         merge_copy(i).start()
@@ -435,14 +439,14 @@
         raw_b(0).start()
         raw_b(1).start()
 
-    down.wait(0)
-    down.go(2, 5)
-    down.wait(1)
-    down.go(3, 6)
-    up.wait(0)
-    up.go(2, 5)
-    up.wait(1)
-    up.go(3, 6)
+    for weights in (down, up):
+        for i in (0, 1):
+            weights.wait(i)
+            weights.go(2 + i)
+    for weights in (down, up):
+        for i in (0, 1):
+            weights.wait(8 + i)
+            weights.go(5 + i)
     for i, k in ((0, 4), (1, 5), (2, 6)):
         merge_arrival(i).wait_recv()
         merge_copy(k).start()
@@ -534,16 +538,23 @@
         def _():
             for q in blocks:
                 G[q, :s] = O0[q]
+
+    def own_gradient(blocks):
+        @pl.when(last)
+        def _():
+            for q in blocks:
                 G[q, s:] = (X[q, s:].astype(F32) + mm(hid[s:], wu[q])).astype(BF)
             back_of(blocks)
 
     leave(order[:4])
+    own_gradient(order[:4])
     up.wait(2, 3)
     up.go(7)
     for i in range(1, nq):
         if i not in FAR:
             norm_copy(i).start()
     leave(order[4:6])
+    own_gradient(order[4:6])
 
     @pl.when(inside)
     def _():
@@ -555,8 +566,7 @@
     def _():
         back_of(order[7:])
 
-    leave(order[6:])
-    nall[d] = N[d, :s]
+    own_gradient(order[6:])
 
     def factor(rows):
         sg, inn = sig[rows], inner[rows]
@@ -578,8 +588,8 @@
         raw_b(4).start()
         raw_b(5).start()
 
-    for first in range(0, nq - 1, 4):
-        group = [bwd_block(j) for j in range(first, min(first + 4, nq - 1))]
+    for first, stop in ((0, 2), (2, nq - 1)):
+        group = [bwd_block(j) for j in range(first, stop)]
         for q in group:
             back = mm_nt(bu[...], wd[q]) * gain_ref[q]
             value = G[q, s:].astype(F32) + scale_b * (back - X[q, s:].astype(F32) * coef_b)
@@ -589,6 +599,11 @@
         def _():
             for q in group:
                 bwd_send(q).start()
+
+        if first == 0:
+            leave(order[6:])
+
+    nall[d] = N[d, :s]
 
     turned = wide_b.T.astype(BF)
     for k in range(RING):
@@ -636,6 +651,49 @@
         ss[:s] += jnp.sum(v * v, -1, keepdims=True)
         ic[...] += mm((v * gain_ref[q]).astype(BF), wd[q])
 
+    def forward_output():
+        scale = lax.rsqrt(ss[:s] * (1.0 / width) + EPS)
+        hid2[...] = swish(ic[...] * scale).astype(BF)
+
+        def finish(q):
+            xin[q] = (xin[q].astype(F32) + mm(hid2[...], wu[q])).astype(BF)
+
+        each(nq, finish)
+        for q in range(nq):
+            fwd_out(q).start()
+
+    def early_sends_done():
+        down.drain()
+        up.drain()
+        for i in range(7):
+            merge_copy(i).wait_send()
+
+        @pl.when(z > 0)
+        def _():
+            text_z(z).wait_send()
+            tok_z(z).wait_send()
+
+        @pl.when((z > 0) & mine)
+        def _():
+            map_z(z).wait_send()
+
+        @pl.when(inside)
+        def _():
+            for i in range(3):
+                raw_f(i).wait_send()
+
+        @pl.when(p > 0)
+        def _():
+            for i in range(6):
+                raw_b(i).wait_send()
+
+        @pl.when(last)
+        def _():
+            raw_b(6).wait_send()
+
+    def in_turn(j):
+        return (p > 0) & ((j < nq - 1) | jnp.logical_not(down_wrap))
+
     def second(j, carry):
         qf, qb = fwd_block(j), jnp.where(j == 0, d, bwd_block(j - 1))
 
@@ -646,7 +704,7 @@
                 tok_y(y + i - 1).wait_recv()
                 tok_y(y + i - 1).start()
 
-        @pl.when((p > 0) & (j > 0))
+        @pl.when(in_turn(j) & (j > 0))
         def _():
             fwd_send(qf).wait_recv()
 
@@ -656,9 +714,13 @@
                 raw_f(i).wait_recv()
             xin[d] = (rx[...].astype(F32) + mm(rh[...], ru[...])).astype(BF)
 
-        @pl.when(p > 0)
+        @pl.when(in_turn(j))
         def _():
             take_forward(qf)
+
+        @pl.when(j == 6)
+        def _():
+            early_sends_done()
 
         @pl.when((j == 4) & (p == 0))
         def _():
@@ -687,17 +749,9 @@
 
             each(nq, assemble)
 
-        @pl.when(j == nq - 1)
-        def _():
-            scale = lax.rsqrt(ss[:s] * (1.0 / width) + EPS)
-            hid2[...] = swish(ic[...] * scale).astype(BF)
-
-            def finish(q):
-                xin[q] = (xin[q].astype(F32) + mm(hid2[...], wu[q])).astype(BF)
-
-            each(nq, finish)
-            for q in range(nq):
-                fwd_out(q).start()
+        @pl.when((j == nq - 1) & jnp.logical_not(down_wrap))
+        def _():
+            forward_output()
 
         @pl.when(inside & (j > 0))
         def _():
@@ -729,7 +783,7 @@
             for i in range(1, nq):
                 but_copy(i).start()
             bu2[...] = bu_a
-            ss[:s] = mean_a
+            ss[s:] = mean_a
 
         term = mm(hidt[...], G[qb])
 
@@ -770,7 +824,7 @@
     lax.fori_loop(0, nq, second, 0)
 
     scale_a = sc[lo_rows]
-    coef_a = scale_a * ss[:s]
+    coef_a = scale_a * ss[s:]
 
     def second_backward(q):
         back = mm_nt(bu2[...], wd[q]) * gain_ref[q]
@@ -780,6 +834,13 @@
     each(nq, second_backward)
     for q in range(nq):
         bwd_out(q).start()
+
+    @pl.when(down_wrap)
+    def _():
+        q = fwd_block(nq - 1)
+        fwd_send(q).wait_recv()
+        take_forward(q)
+        forward_output()
 
     for k in (1, 2):
         up_x(k).wait_recv()
@@ -792,30 +853,17 @@
     up_out.start()
     for k in (1, 2):
         down_x(k).wait_recv()
-    for i in range(1, nq):
+    total = accd[...] + mm(but[d], nall[d])
+    for k in (1, 2):
+        total += dxr[k].astype(F32)
+    for i in sorted(range(1, nq), key=lambda i: abs(i - nq // 2), reverse=True):
         norm_arrival(i).wait_recv()
         but_arrival(i).wait_recv()
-    total = accd[...]
-    for k in (1, 2):
-        total += dxr[k].astype(F32)
-    for q in range(nq):
+        q = (d + nq - i) % nq
         total += mm(but[q], nall[q])
     gdo[...] = total.T
     down_out = pltpu.make_async_copy(gdo, gd_h, outs.at[2 * nq + 1])
     down_out.start()
-
-    down.drain()
-    up.drain()
-    for i in range(7):
-        merge_copy(i).wait_send()
-    @pl.when(z > 0)
-    def _():
-        text_z(z).wait_send()
-        tok_z(z).wait_send()
-
-    @pl.when((z > 0) & mine)
-    def _():
-        map_z(z).wait_send()
 
     @pl.when((z == 0) & (y > 0))
     def _():
@@ -855,20 +903,6 @@
         return carry
 
     lax.fori_loop(0, nq, drain, 0)
-
-    @pl.when(inside)
-    def _():
-        for i in range(3):
-            raw_f(i).wait_send()
-
-    @pl.when(p > 0)
-    def _():
-        for i in range(6):
-            raw_b(i).wait_send()
-
-    @pl.when(last)
-    def _():
-        raw_b(6).wait_send()
 
     up_out.wait()
     down_out.wait()
@@ -952,7 +986,7 @@
         vm((s, r), BF),
         vm((db, r), F32),
         dma(8 + 3 * nq),
-        dma(8), dma(8), dma(8), dma(8), dma(7), dma(7),
+        dma(10), dma(10), dma(10), dma(10), dma(7), dma(7),
         dma(nq), dma(nq), dma(nq), dma(nq),
         dma(nq), dma(nq), dma(nq), dma(nq),
         dma(RING), dma(RING), dma(RING), dma(RING),

time: 92.5 us -> 91.6 us (level)
  no operation moved by 1% of the time
where the time goes in v4:
time: 91.6 us; the launch traced here: 90 us
  Pallas kernels  87.9 us (96%)
  between operations  2.1 us (2%)
    pallas_call x1, Pallas kernels, body(): pl.pallas_call(functools.partial(kernel, n_pipe), out_shape=(jax.ShapeDty...  83.2 us
    pallas_call x1, Pallas kernels, body(): pl.pallas_call(hand_over, out_shape=(jax.ShapeDtypeStruct((1, 1, s, width...  4.66 us

profile of v4, /device:TPU:1, one launch (start us, length us, event | category | flops | bytes accessed | tf_op | source)
XLA Modules:
  0.0 90.0 jit_solution(2007311704150726079)
XLA Ops:
  1.9 83.2 %relay.1 = (bf16[128,8192]{1,0:T(8,128)(2,1)}, bf16[128,8192]{1,0:T(8,128)(2,1)}, f32[1024,128]{1,0:T(8,128)}, f32[128,1024]{1,0:T(8,128)}) custom-call(bf16[128,8192]{1,0:T(8,128)(2,1)} %bitcast.11, bf16[128,8192]{1,0:T(8,128)(2,1)} %bitcast.12, bf16[128,8192]{1,0:T(8,128)(2,1)} %bitcast.13, bf16[128,256]{1,0:T(8,128)(2,1)} %bitcast.19, ...), custom_call_target="tpu_custom_call" | custom-call | tf_op jit(solution)/shard_map/relay/pallas_call | solution.py:1001
  85.1 4.7 %hand_over.1 = (bf16[1,1,128,8192]{3,2,1,0:T(8,128)(2,1)}, bf16[1,1,128,8192]{3,2,1,0:T(8,128)(2,1)}, f32[1,1024,128]{2,1,0:T(8,128)}, f32[1,128,1024]{2,1,0:T(8,128)}) custom-call(bf16[128,8192]{1,0:T(8,128)(2,1)} %get-tuple-element.8.refs_0_, bf16[128,8192]{1,0:T(8,128)(2,1)} %get-tuple-element.9.refs_1_, f32[1024,128]{1,0:T(8,128)} %get-tuple-element.10.refs_2_, ...), custom_call_target="tpu_custom_call" | custom-call | tf_op jit(solution)/shard_map/hand_over/pallas_call | solution.py:1024

commit v5 on v4

--- a/solution.py
+++ b/solution.py
@@ -242,7 +242,7 @@
         return to_row(ref, ref, tzs, tzr, slot)
 
     def to_first(ref, send, recv, slot_y):
-        target = jnp.where(y == n_y - 1, 0, y - 1) * Z
+        target = jnp.where(y == n_y - 1, 0, jnp.maximum(y - 1, 0)) * Z
         return rcopy(ref, ref, send.at[slot_y], recv.at[slot_y], (target, d))
 
     def text_y(slot):
@@ -259,11 +259,13 @@
 
     mine = z % 2 == c
 
+    ahead, behind = ((p + 1) % n_pipe, d), ((p + n_pipe - 1) % n_pipe, d)
+
     def fwd_send(q):
-        return rcopy(O0.at[q], xin.at[q], zfs.at[q], zfr.at[q], (p + 1, d))
+        return rcopy(O0.at[q], xin.at[q], zfs.at[q], zfr.at[q], ahead)
 
     def bwd_send(q):
-        return rcopy(B0.at[q], G.at[q, pl.ds(0, s)], zbs.at[q], zbr.at[q], (p - 1, d))
+        return rcopy(B0.at[q], G.at[q, pl.ds(0, s)], zbs.at[q], zbr.at[q], behind)
 
     def raw_f(i):
         src, dst = (
@@ -271,7 +273,7 @@
             lambda: (wu.at[d], ru),
             lambda: (hid.at[pl.ds(0, s)], rh),
         )[i]()
-        return rcopy(src, dst, rfs.at[i], rfr.at[i], (p + 1, d))
+        return rcopy(src, dst, rfs.at[i], rfr.at[i], ahead)
 
     def raw_b(i):
         src, dst = (
@@ -283,10 +285,10 @@
             lambda: (pk, rp),
             lambda: (hid.at[pl.ds(s, s)], rb.at[pl.ds(s, s)]),
         )[i]()
-        return rcopy(src, dst, rbs.at[i], rbr.at[i], (p - 1, d))
+        return rcopy(src, dst, rbs.at[i], rbr.at[i], behind)
 
     def raw_u():
-        return rcopy(wu.at[d], rg, rbs.at[1], rbr.at[1], (p - 1, d))
+        return rcopy(wu.at[d], rg, rbs.at[1], rbr.at[1], behind)
 
     def fwd_block(j):
         return at((x + pick(j // 2, FWD)) % RING, jnp.where(j % 2 == 0, c, 1 - c))

time: 91.6 us -> 91.6 us (level)
  no operation moved by 1% of the time
where the time goes in v5:
time: 91.6 us; the launch traced here: 90 us
  Pallas kernels  87.9 us (96%)
  between operations  2.1 us (2%)
    pallas_call x1, Pallas kernels, body(): pl.pallas_call(functools.partial(kernel, n_pipe), out_shape=(jax.ShapeDty...  83.2 us
    pallas_call x1, Pallas kernels, body(): pl.pallas_call(hand_over, out_shape=(jax.ShapeDtypeStruct((1, 1, s, width...  4.66 us

profile of v5, /device:TPU:1, one launch (start us, length us, event | category | flops | bytes accessed | tf_op | source)
XLA Modules:
  0.0 90.0 jit_solution(14359113773771080986)
XLA Ops:
  1.9 83.2 %relay.1 = (bf16[128,8192]{1,0:T(8,128)(2,1)}, bf16[128,8192]{1,0:T(8,128)(2,1)}, f32[1024,128]{1,0:T(8,128)}, f32[128,1024]{1,0:T(8,128)}) custom-call(bf16[128,8192]{1,0:T(8,128)(2,1)} %bitcast.11, bf16[128,8192]{1,0:T(8,128)(2,1)} %bitcast.12, bf16[128,8192]{1,0:T(8,128)(2,1)} %bitcast.13, bf16[128,256]{1,0:T(8,128)(2,1)} %bitcast.19, ...), custom_call_target="tpu_custom_call" | custom-call | tf_op jit(solution)/shard_map/relay/pallas_call | solution.py:1003
  85.1 4.7 %hand_over.1 = (bf16[1,1,128,8192]{3,2,1,0:T(8,128)(2,1)}, bf16[1,1,128,8192]{3,2,1,0:T(8,128)(2,1)}, f32[1,1024,128]{2,1,0:T(8,128)}, f32[1,128,1024]{2,1,0:T(8,128)}) custom-call(bf16[128,8192]{1,0:T(8,128)(2,1)} %get-tuple-element.8.refs_0_, bf16[128,8192]{1,0:T(8,128)(2,1)} %get-tuple-element.9.refs_1_, f32[1024,128]{1,0:T(8,128)} %get-tuple-element.10.refs_2_, ...), custom_call_target="tpu_custom_call" | custom-call | tf_op jit(solution)/shard_map/hand_over/pallas_call | solution.py:1026
